TPU v7x, 256 devices: a whole 4x4x8 slice. The times are simulated.
256 devices in a mesh: region: 4 (over y), dom: 64 (over x, z, core).
Axes of the slice: x: 4, y: 4, z: 8, core: 2. Of those that a mesh axis runs over, the one named last changes fastest.
Arguments:
- features: bfloat16 [65536, 768], P(('region', 'dom')), may hold values from -6 to 6
- cotangent: bfloat16 [65536, 768], P(('region', 'dom')), may hold values from -6 to 6
- conv_weight: bfloat16 [2, 64, 128], replicated, may hold values from -0.5 to 0.5
- conv_bias: float32 [128], replicated, may hold values from -3 to 3
- diff_weight: bfloat16 [3, 64, 64], replicated, may hold values from -0.75 to 0.75
- edge_tiles: bfloat16 [3072, 128, 128], P(('region', 'dom')), may hold values from -0.21875 to 0.21875
- tile_source: int32 [256, 12], P(('region', 'dom')), may hold values from 0 to 9, as said below
- tile_target: int32 [256, 12], P(('region', 'dom')), may hold values from 0 to 1
- tile_count: int32 [256], P(('region', 'dom')), may hold values from 5 to 12, as said below
Outputs:
- mixed: bfloat16 [65536, 768], P(('region', 'dom'))
- grad_features: bfloat16 [65536, 768], P(('region', 'dom'))
- grad_diff: float32 [3, 64, 64], replicated
- grad_conv: float32 [2, 64, 128], replicated
- grad_bias: float32 [128], replicated
Inputs may be any that keep to these rules, and one draw needn't show every extreme that they name: `tile_source`: s // 2 chooses the device itself, its lower or upper neighbour along dom, or its lower or upper neighbour along region; s % 2 is a block of that device; the first five slots of each device name five different choices of neighbour. `tile_count`: slots at or past the count are not part of the graph; some devices use all 12 slots.
All inputs are finite; a program needn't handle non-finite values.
Results may differ from a plain program's by a relative error of at most 0.0055.
Values may be sent and summed in bfloat16 or wider, within the bound.
No kernel may reach another device: no remote copies, remote signals or barrier semaphores. Data moves between devices by JAX's collectives and lax.ppermute only.
A program may use at most 128 MiB of HBM per device.

v0:
```python
import math

import jax
import jax.numpy as jnp
from jax import lax
from jax.sharding import PartitionSpec as P

PLACES = ((1, 1), (1, 0), (1, 2), (0, 1), (2, 1))


def padded(block, sides, width):
    for axis, dim in sides:
        count = lax.axis_size(axis)
        forward = [(i, i + 1) for i in range(count - 1)]
        forward.append((count - 1, 0))
        backward = [(target, source) for source, target in forward]
        low = lax.ppermute(
            lax.slice_in_dim(block, block.shape[dim] - width, None, axis=dim), axis, forward
        )
        high = lax.ppermute(lax.slice_in_dim(block, 0, width, axis=dim), axis, backward)
        block = jnp.concatenate([low, block, high], axis=dim)
    return block


def from_behind(block, axis, distance):
    devices = range(lax.axis_size(axis))
    route = [((i - distance) % len(devices), i) for i in devices]
    return lax.ppermute(block, axis, route)


def assign_slots(totals, products, bucket_slice, live_slice):
    kept = jnp.where(live_slice[:, None, None], products, 0.0)
    return totals.at[bucket_slice].add(kept)


def run_tiles(slot_products, bucket_ids, live_mask, slot_total, group_size, initial):
    totals = initial
    for which in range(slot_total // group_size):
        offset = which * group_size
        products = slot_products(offset)
        bucket_slice = lax.dynamic_slice_in_dim(bucket_ids, offset, group_size)
        live_slice = lax.dynamic_slice_in_dim(live_mask, offset, group_size)
        totals = assign_slots(totals, products, bucket_slice, live_slice)
    return totals


def neighbour_stack(rims, block_count, block_rows, feat_width):
    pieces = [
        rims[region_pos, dom_pos].reshape(block_count, block_rows, feat_width)
        for region_pos, dom_pos in PLACES
    ]
    return jnp.concatenate(pieces, axis=0)


def forward_hop(field, edge_tiles, source_ids, target_ids, count):
    block_count, block_rows, feat_width = field.shape
    slot_total = edge_tiles.shape[0]
    rims = padded(field.reshape(1, 1, -1), (("region", 0), ("dom", 1)), 1)
    sources = neighbour_stack(rims, block_count, block_rows, feat_width)

    def slot_products(offset):
        tiles = lax.dynamic_slice_in_dim(edge_tiles, offset, block_count, 0)
        wanted = lax.dynamic_slice_in_dim(source_ids, offset, block_count)
        source_rows = jnp.take(sources, wanted, axis=0)
        return jnp.einsum("sij,sjf->sif", tiles, source_rows, preferred_element_type=jnp.float32)

    live_mask = jnp.arange(slot_total, dtype=jnp.int32) < count
    initial = jnp.zeros((block_count, block_rows, feat_width), jnp.float32)
    return run_tiles(slot_products, target_ids, live_mask, slot_total, block_count, initial)


def push_back(field, edge_tiles, source_ids, target_ids, count):
    block_count, block_rows, feat_width = field.shape
    slot_total = edge_tiles.shape[0]

    def slot_products(offset):
        tiles = lax.dynamic_slice_in_dim(edge_tiles, offset, block_count, 0)
        wanted = lax.dynamic_slice_in_dim(target_ids, offset, block_count)
        own_rows = jnp.take(field, wanted, axis=0)
        return jnp.einsum("sji,sjf->sif", tiles, own_rows, preferred_element_type=jnp.float32)

    live_mask = jnp.arange(slot_total, dtype=jnp.int32) < count
    initial = jnp.zeros((5 * block_count, block_rows, feat_width), jnp.float32)
    buckets = run_tiles(slot_products, source_ids, live_mask, slot_total, block_count, initial)
    buckets = buckets.reshape(5, block_count, block_rows, feat_width)
    totals = buckets[0]
    totals = totals + from_behind(buckets[1], "dom", -1)
    totals = totals + from_behind(buckets[2], "dom", 1)
    totals = totals + from_behind(buckets[3], "region", -1)
    totals = totals + from_behind(buckets[4], "region", 1)
    return totals


def channel_mix(left, right):
    return jnp.einsum("nti,io->nto", left, right, preferred_element_type=jnp.float32)


def channel_back(left, right):
    return jnp.einsum("nto,io->nti", left, right, preferred_element_type=jnp.float32)


def outer_sum(left, right):
    return jnp.einsum("nti,nto->io", left, right, preferred_element_type=jnp.float32)


def local(
    features,
    cotangent,
    conv_weight,
    conv_bias,
    diff_weight,
    edge_tiles,
    tile_source,
    tile_target,
    tile_count,
):
    cell_count, feat_width = features.shape
    channels = conv_weight.shape[1]
    steps_total = feat_width // channels
    block_rows = edge_tiles.shape[1]
    block_count = cell_count // block_rows
    source_ids = tile_source[0]
    target_ids = tile_target[0]
    count = tile_count[0]

    def as_blocks(field):
        return field.reshape(block_count, block_rows, feat_width)

    def as_cells(field):
        return field.reshape(cell_count, steps_total, channels)

    inputs = features.reshape(cell_count, steps_total, channels)
    earlier = jnp.concatenate(
        [jnp.zeros((cell_count, 1, channels), inputs.dtype), inputs[:, :-1]], axis=1
    )
    pre = channel_mix(inputs, conv_weight[0]) + channel_mix(earlier, conv_weight[1]) + conv_bias
    filt = jnp.tanh(pre[..., :channels])
    opened = jax.nn.sigmoid(pre[..., channels:])
    gated = (filt * opened).astype(jnp.bfloat16)
    hop_one = as_cells(
        forward_hop(as_blocks(gated), edge_tiles, source_ids, target_ids, count)
    ).astype(jnp.bfloat16)
    hop_two = as_cells(
        forward_hop(as_blocks(hop_one), edge_tiles, source_ids, target_ids, count)
    ).astype(jnp.bfloat16)
    mixed = (
        inputs.astype(jnp.float32)
        + channel_mix(gated, diff_weight[0])
        + channel_mix(hop_one, diff_weight[1])
        + channel_mix(hop_two, diff_weight[2])
    )
    mixed = mixed.astype(jnp.bfloat16).reshape(cell_count, feat_width)

    def adjoint_hop(field):
        return as_cells(push_back(as_blocks(field), edge_tiles, source_ids, target_ids, count))

    upstream = cotangent.reshape(cell_count, steps_total, channels)
    back_two = channel_back(upstream, diff_weight[2]).astype(jnp.bfloat16)
    back_one = (channel_back(upstream, diff_weight[1]) + adjoint_hop(back_two)).astype(jnp.bfloat16)
    back_zero = channel_back(upstream, diff_weight[0]) + adjoint_hop(back_one)
    back_filter = back_zero * opened * (1.0 - filt * filt)
    back_gate = back_zero * filt * opened * (1.0 - opened)
    back_pre = jnp.concatenate([back_filter, back_gate], axis=-1).astype(jnp.bfloat16)
    later = jnp.concatenate(
        [back_pre[:, 1:], jnp.zeros((cell_count, 1, 2 * channels), back_pre.dtype)], axis=1
    )
    grad_features = (
        upstream.astype(jnp.float32)
        + channel_back(back_pre, conv_weight[0])
        + channel_back(later, conv_weight[1])
    )
    grad_features = grad_features.astype(jnp.bfloat16).reshape(cell_count, feat_width)
    local_diff = jnp.stack(
        [outer_sum(gated, upstream), outer_sum(hop_one, upstream), outer_sum(hop_two, upstream)]
    )
    local_conv = jnp.stack([outer_sum(inputs, back_pre), outer_sum(earlier, back_pre)])
    local_bias = jnp.sum(back_pre.astype(jnp.float32), axis=(0, 1))
    summed_diff, summed_conv, summed_bias = lax.psum(
        (local_diff, local_conv, local_bias), ("region", "dom")
    )
    scale = 1.0 / math.sqrt(cell_count * lax.axis_size(("region", "dom")) * steps_total)
    return (mixed, grad_features, summed_diff * scale, summed_conv * scale, summed_bias * scale)


def solution(mesh):
    in_specs = (
        P(("region", "dom"), None),
        P(("region", "dom"), None),
        P(),
        P(),
        P(),
        P(("region", "dom"), None, None),
        P(("region", "dom"), None),
        P(("region", "dom"), None),
        P(("region", "dom")),
    )
    out_specs = (P(("region", "dom"), None), P(("region", "dom"), None), P(), P(), P())
    return jax.shard_map(local, mesh=mesh, in_specs=in_specs, out_specs=out_specs, check_vma=False)
```

profile of v0, /device:TPU:1, one launch (start us, length us, event | category | flops | bytes accessed | tf_op | source)
XLA Modules:
  0.0 709.6 jit_solution(5765344912624325155)
XLA Ops:
  19.4 2.3 copy.193
  23.6 2.3 copy.196
  28.4 2.3 copy.199
  33.6 2.2 broadcast.279.clone
  35.8 2.8 scatter_fusion.12
  38.6 2.8 scatter_fusion.13
  41.5 2.8 scatter_fusion.14
  44.3 2.8 scatter_fusion.15
  47.1 2.8 scatter_fusion.16
  49.9 2.8 scatter_fusion.17
  52.7 3.4 fusion.196
  56.1 3.6 collective-permute-start.10
  64.3 11.8 %collective-permute-done.10 = f32[2,128,768]{2,1,0:T(8,128)S(1)} collective-permute-done((f32[2,128,768]{2,1,0:T(8,128)}, f32[2,128,768]{2,1,0:T(8,128)S(1)}, u32[]{:S(2)}, u32[]{:S(2)}) %collective-permute-start.10) | collective-permute-done | bytes 786464 | tf_op jit(solution)/shard_map/ppermute | solution.py:28
  76.1 3.1 collective-permute-done.11
  93.0 2.3 fusion.4
  98.6 2.3 copy.212
  100.9 2.3 fusion.2
  103.2 2.3 copy.215
  107.5 2.3 copy.218
  111.6 2.3 copy.221
  114.0 2.2 broadcast.279
  116.2 2.8 scatter_fusion.18
  119.0 2.8 scatter_fusion.19
  121.8 2.8 scatter_fusion.20
  124.7 2.8 scatter_fusion.21
  127.5 2.8 scatter_fusion.22
  130.3 2.8 scatter_fusion.23
  133.1 2.2 fusion.195
  135.3 3.6 collective-permute-start.12
  138.9 2.8 collective-permute-start.14
  144.6 4.2 collective-permute-done.12
  148.7 7.6 %collective-permute-done.14 = f32[2,128,768]{2,1,0:T(8,128)S(1)} collective-permute-done((f32[2,128,768]{2,1,0:T(8,128)S(1)}, f32[2,128,768]{2,1,0:T(8,128)S(1)}, u32[]{:S(2)}, u32[]{:S(2)}) %collective-permute-start.14) | collective-permute-done | bytes 786464 | tf_op jit(solution)/shard_map/ppermute | solution.py:28
  156.3 3.3 collective-permute-done.15
  162.2 2.6 reshape.444
  169.1 2.7 collective-permute-start.1
  173.6 12.5 %collective-permute-done = bf16[1,1,196608]{2,1,0:T(2,128)(2,1)S(1)} collective-permute-done((bf16[1,1,196608]{2,1,0:T(2,128)(2,1)}, bf16[1,1,196608]{2,1,0:T(2,128)(2,1)S(1)}, u32[]{:S(2)}, u32[]{:S(2)}) %collective-permute-start) | collective-permute-done | bytes 393248 | tf_op jit(solution)/shard_map/ppermute | solution.py:17
  187.1 5.5 pad_maximum_fusion
  192.6 4.2 copy.147
  196.7 5.2 collective-permute-start.2
  209.5 8.2 %reduce.2 = bf16[196608]{0:T(1024)(128)(2,1)S(1)} reduce(bf16[1,1,196608]{2,1,0:T(2,128)(2,1)S(1)} %collective-permute-done, bf16[]{:T(256)} %constant.17), dimensions={0,1}, to_apply=%ppermute.48.reduce_sub_computation | reduce | bytes 786434 | tf_op jit(solution)/shard_map/ppermute | solution.py:17
  218.1 8.2 %reduce.3 = bf16[196608]{0:T(1024)(128)(2,1)S(1)} reduce(bf16[1,1,196608]{2,1,0:T(2,128)(2,1)S(1)} %copy-done.22, bf16[]{:T(256)} %constant.17), dimensions={0,1}, to_apply=%ppermute.49.reduce_sub_computation | reduce | bytes 786434 | tf_op jit(solution)/shard_map/ppermute | solution.py:20
  226.6 7.7 %slice_reduce_fusion.3 = bf16[196608]{0:T(1024)(128)(2,1)S(1)} fusion(bf16[3,1,196608]{2,0,1:T(4,128)(2,1)} %collective-permute-done.2), kind=kLoop, calls=%fused_computation.127 | loop fusion | bytes 786432 | tf_op jit(solution)/shard_map/slice | solution.py:49
  234.7 7.9 %slice_reduce_fusion.2 = bf16[196608]{0:T(1024)(128)(2,1)S(1)} fusion(bf16[3,1,196608]{2,0,1:T(4,128)(2,1)} %collective-permute-done.3), kind=kLoop, calls=%fused_computation.126 | loop fusion | bytes 786432 | tf_op jit(solution)/shard_map/slice | solution.py:49
  246.0 2.2 gather_fusion
  253.3 2.2 gather_fusion.2
  257.8 2.2 gather_fusion.3
  262.2 2.2 gather_fusion.4
  266.7 2.2 gather_fusion.5
  282.1 2.7 collective-permute-start.5
  286.2 11.6 %collective-permute-done.4 = bf16[1,1,196608]{2,0,1:T(2,128)(2,1)S(1)} collective-permute-done((bf16[1,1,196608]{2,0,1:T(2,128)(2,1)}, bf16[1,1,196608]{2,0,1:T(2,128)(2,1)S(1)}, u32[]{:S(2)}, u32[]{:S(2)}) %collective-permute-start.4) | collective-permute-done | bytes 393248 | tf_op jit(solution)/shard_map/ppermute | solution.py:17
  297.9 4.9 pad_maximum_fusion.1
  302.8 6.9 collective-permute-start.6
  313.7 235.5 %all-reduce.5.cloned.1.call-done = f32[2,64,128]{2,1,0:T(8,128)} async-done(((f32[2,64,128]{2,1,0:T(8,128)}), f32[2,64,128]{2,1,0:T(8,128)}) %all-reduce.5.cloned.1.call-update) | async-done | bytes 65552 | tf_op jit(solution)/shard_map/psum | solution.py:178
  554.6 8.2 %reduce.6 = bf16[196608]{0:T(1024)(128)(2,1)S(1)} reduce(bf16[1,1,196608]{2,0,1:T(2,128)(2,1)S(1)} %copy-done.28, bf16[]{:T(256)} %constant.17), dimensions={0,1}, to_apply=%ppermute.52.reduce_sub_computation | reduce | bytes 786434 | tf_op jit(solution)/shard_map/ppermute | solution.py:17
  563.1 8.2 %reduce.7 = bf16[196608]{0:T(1024)(128)(2,1)S(1)} reduce(bf16[1,1,196608]{2,0,1:T(2,128)(2,1)S(1)} %copy-done.26, bf16[]{:T(256)} %constant.17), dimensions={0,1}, to_apply=%ppermute.53.reduce_sub_computation | reduce | bytes 786434 | tf_op jit(solution)/shard_map/ppermute | solution.py:20
  571.6 7.7 %slice_reduce_fusion.1 = bf16[196608]{0:T(1024)(128)(2,1)S(1)} fusion(bf16[3,1,196608]{2,0,1:T(4,128)(2,1)} %collective-permute-done.6), kind=kLoop, calls=%fused_computation.125 | loop fusion | bytes 786432 | tf_op jit(solution)/shard_map/slice | solution.py:49
  579.7 7.9 %slice_reduce_fusion = bf16[196608]{0:T(1024)(128)(2,1)S(1)} fusion(bf16[3,1,196608]{2,0,1:T(4,128)(2,1)} %collective-permute-done.7), kind=kLoop, calls=%fused_computation.124 | loop fusion | bytes 786432 | tf_op jit(solution)/shard_map/slice | solution.py:49
  591.0 2.2 gather_fusion.6
  593.3 2.2 gather_fusion.7
  595.5 3.0 gather_fusion.8
  598.5 3.0 gather_fusion.9
  601.5 3.0 gather_fusion.10
  604.5 2.2 gather_fusion.11
  624.4 75.1 %all-reduce.2 = (f32[3,64,64]{2,1,0:T(8,128)S(1)}, f32[128]{0:T(128)S(1)}) all-reduce(f32[3,64,64]{2,1,0:T(8,128)S(1)} %pad_maximum_fusion.3, f32[128]{0:T(128)S(1)} %copy-done.87), channel_id=1, replica_groups=mesh['region'=4,'dom'=64] {'region','dom'}, use_global_device_ids=true, to_apply=%region_24.27 | all-reduce | flops 12416 | bytes 99328 | tf_op jit(solution)/shard_map/psum | solution.py:178
  (341 shorter events, 128.6 us)
Async XLA Ops:
  7.2 542.0 %all-reduce.5.cloned.1.call-start = ((), (), s32[]{:S(2)}) async-start(), calls=%async_computation | async-start | bytes 131072 | tf_op jit(solution)/shard_map/psum | solution.py:178
  8.7 4.2 copy-start.81
  8.7 6.2 copy-start.78
  8.7 9.5 %copy-start.75 = (pred[2]{0:T(512)(128)(4,1)}, pred[2]{0:T(512)(128)(4,1)S(1)}, u32[]{:S(2)}) copy-start(pred[2]{0:T(512)(128)(4,1)S(1)} %get-tuple-element.65) | copy-start | bytes 10
  8.7 13.6 %copy-start.70 = (pred[2]{0:T(512)(128)(4,1)}, pred[2]{0:T(512)(128)(4,1)S(1)}, u32[]{:S(2)}) copy-start(pred[2]{0:T(512)(128)(4,1)S(1)} %get-tuple-element.67) | copy-start | bytes 10
  8.7 18.4 %copy-start.69 = (pred[2]{0:T(512)(128)(4,1)}, pred[2]{0:T(512)(128)(4,1)S(1)}, u32[]{:S(2)}) copy-start(pred[2]{0:T(512)(128)(4,1)S(1)} %get-tuple-element.69) | copy-start | bytes 10
  12.2 5.9 copy-start.40
  17.5 4.8 copy-start.51
  17.5 4.8 copy-start.52
  26.5 4.2 copy-start.53
  35.8 5.6 copy-start.7
  35.8 5.6 copy-start.79
  38.6 5.6 copy-start.8
  38.6 5.6 copy-start.76
  41.4 5.6 copy-start.17
  41.4 5.6 copy-start.73
  44.3 5.6 copy-start.20
  44.3 5.6 copy-start.71
  52.7 9.6 %copy-start.31 = (bf16[256,768]{1,0:T(8,128)(2,1)S(1)}, bf16[256,768]{1,0:T(8,128)(2,1)}, u32[]{:S(2)}) copy-start(bf16[256,768]{1,0:T(8,128)(2,1)} %param.13) | copy-start | bytes 1179652
  56.1 20.0 %collective-permute-start.10 = (f32[2,128,768]{2,1,0:T(8,128)}, f32[2,128,768]{2,1,0:T(8,128)S(1)}, u32[]{:S(2)}, u32[]{:S(2)}) collective-permute-start(f32[2,128,768]{2,1,0:T(8,128)} %get-tuple-element.56), channel_id=1, source_target_pairs={{64,0},{128,64},{192,128},{0,192},{65,1},{129,65},{193,129},{1,193... | collective-permute-start | bytes 2359304 | tf_op jit(solution)/shard_map/ppermute | solution.py:28
  59.7 19.6 %collective-permute-start.11 = (f32[2,128,768]{2,1,0:T(8,128)}, f32[2,128,768]{2,1,0:T(8,128)}, u32[]{:S(2)}, u32[]{:S(2)}) collective-permute-start(f32[2,128,768]{2,1,0:T(8,128)} %get-tuple-element.55), channel_id=1, source_target_pairs={{192,0},{0,64},{64,128},{128,192},{193,1},{1,65},{65,129},{129,193... | collective-permute-start | bytes 2359304 | tf_op jit(solution)/shard_map/ppermute | solution.py:28
  59.7 19.6 %collective-permute-start.8 = (f32[2,128,768]{2,1,0:T(8,128)}, f32[2,128,768]{2,1,0:T(8,128)}, u32[]{:S(2)}, u32[]{:S(2)}) collective-permute-start(f32[2,128,768]{2,1,0:T(8,128)} %get-tuple-element.54), channel_id=1, source_target_pairs={{1,0},{2,1},{3,2},{4,3},{5,4},{6,5},{7,6},{8,7},{9,8},{10,9},{11,1... | collective-permute-start | bytes 2359304 | tf_op jit(solution)/shard_map/ppermute | solution.py:28
  61.3 17.9 %collective-permute-start.9 = (f32[2,128,768]{2,1,0:T(8,128)S(1)}, f32[2,128,768]{2,1,0:T(8,128)}, u32[]{:S(2)}, u32[]{:S(2)}) collective-permute-start(f32[2,128,768]{2,1,0:T(8,128)S(1)} %get-tuple-element.57), channel_id=1, source_target_pairs={{63,0},{0,1},{1,2},{2,3},{3,4},{4,5},{5,6},{6,7},{7,8},{8,9},{9,10... | collective-permute-start | bytes 2359304 | tf_op jit(solution)/shard_map/ppermute | solution.py:28
  62.4 81.7 %copy-start.5 = (bf16[256,768]{0,1:T(8,128)(2,1)}, bf16[256,768]{0,1:T(8,128)(2,1)S(1)}, u32[]{:S(2)}) copy-start(bf16[256,768]{0,1:T(8,128)(2,1)S(1)} %copy.144) | copy-start | bytes 1179652
  85.8 6.5 copy-start.45
  85.8 6.5 copy-start.82
  98.6 6.9 copy-start.29
  116.2 5.6 copy-start.80
  119.0 5.6 copy-start.77
  121.8 5.6 copy-start.74
  124.6 5.6 copy-start.72
  133.1 10.6 %copy-start.32 = (bf16[2,64,128]{2,1,0:T(8,128)(2,1)S(1)}, bf16[2,64,128]{2,1,0:T(8,128)(2,1)}, u32[]{:S(2)}) copy-start(bf16[2,64,128]{2,1,0:T(8,128)(2,1)} %param.15) | copy-start | bytes 98308
  135.3 8.8 %copy-start.88 = (f32[128]{0:T(128)S(1)}, f32[128]{0:T(128)}, u32[]{:S(2)}) copy-start(f32[128]{0:T(128)} %param.16) | copy-start | bytes 1540
  135.3 13.4 %collective-permute-start.12 = (f32[2,128,768]{2,1,0:T(8,128)S(1)}, f32[2,128,768]{2,1,0:T(8,128)S(1)}, u32[]{:S(2)}, u32[]{:S(2)}) collective-permute-start(f32[2,128,768]{2,1,0:T(8,128)S(1)} %get-tuple-element.50), channel_id=1, source_target_pairs={{1,0},{2,1},{3,2},{4,3},{5,4},{6,5},{7,6},{8,7},{9,8},{10,9},{11,1... | collective-permute-start | bytes 2359304 | tf_op jit(solution)/shard_map/ppermute | solution.py:28
  138.9 9.8 %collective-permute-start.13 = (f32[2,128,768]{2,1,0:T(8,128)S(1)}, f32[2,128,768]{2,1,0:T(8,128)S(1)}, u32[]{:S(2)}, u32[]{:S(2)}) collective-permute-start(f32[2,128,768]{2,1,0:T(8,128)S(1)} %get-tuple-element.53), channel_id=1, source_target_pairs={{63,0},{0,1},{1,2},{2,3},{3,4},{4,5},{5,6},{6,7},{7,8},{8,9},{9,10... | collective-permute-start | bytes 2359304 | tf_op jit(solution)/shard_map/ppermute | solution.py:28
  138.9 17.4 %collective-permute-start.14 = (f32[2,128,768]{2,1,0:T(8,128)S(1)}, f32[2,128,768]{2,1,0:T(8,128)S(1)}, u32[]{:S(2)}, u32[]{:S(2)}) collective-permute-start(f32[2,128,768]{2,1,0:T(8,128)S(1)} %get-tuple-element.52), channel_id=1, source_target_pairs={{64,0},{128,64},{192,128},{0,192},{65,1},{129,65},{193,129},{1,193... | collective-permute-start | bytes 2359304 | tf_op jit(solution)/shard_map/ppermute | solution.py:28
  141.7 18.0 %collective-permute-start.15 = (f32[2,128,768]{2,1,0:T(8,128)S(1)}, f32[2,128,768]{2,1,0:T(8,128)S(1)}, u32[]{:S(2)}, u32[]{:S(2)}) collective-permute-start(f32[2,128,768]{2,1,0:T(8,128)S(1)} %get-tuple-element.51), channel_id=1, source_target_pairs={{192,0},{0,64},{64,128},{128,192},{193,1},{1,65},{65,129},{129,193... | collective-permute-start | bytes 2359304 | tf_op jit(solution)/shard_map/ppermute | solution.py:28
  166.7 41.7 %copy-start.1 = (bf16[256,12,64]{0,2,1:T(8,128)(2,1)}, bf16[256,12,64]{0,2,1:T(8,128)(2,1)S(1)}, u32[]{:S(2)}) copy-start(bf16[256,12,64]{0,2,1:T(8,128)(2,1)S(1)} %get-tuple-element.58) | copy-start | bytes 1179652
  166.7 41.7 %copy-start.3 = (bf16[256,12,64]{0,2,1:T(8,128)(2,1)}, bf16[256,12,64]{0,2,1:T(8,128)(2,1)S(1)}, u32[]{:S(2)}) copy-start(bf16[256,12,64]{0,2,1:T(8,128)(2,1)S(1)} %get-tuple-element.59) | copy-start | bytes 1179652
  169.0 17.1 %collective-permute-start = (bf16[1,1,196608]{2,1,0:T(2,128)(2,1)}, bf16[1,1,196608]{2,1,0:T(2,128)(2,1)S(1)}, u32[]{:S(2)}, u32[]{:S(2)}) collective-permute-start(bf16[1,1,196608]{2,1,0:T(2,128)(2,1)} %reshape_reshape.4), channel_id=1, source_target_pairs={{0,64},{64,128},{128,192},{192,0},{1,65},{65,129},{129,193},{193,1... | collective-permute-start | bytes 1179656 | tf_op jit(solution)/shard_map/ppermute | solution.py:17
  169.1 17.1 %collective-permute-start.1 = (bf16[1,1,196608]{2,1,0:T(2,128)(2,1)}, bf16[1,1,196608]{2,1,0:T(2,128)(2,1)S(1)}, u32[]{:S(2)}, u32[]{:S(2)}) collective-permute-start(bf16[1,1,196608]{2,1,0:T(2,128)(2,1)} %reshape_reshape.4), channel_id=1, source_target_pairs={{64,0},{128,64},{192,128},{0,192},{65,1},{129,65},{193,129},{1,193... | collective-permute-start | bytes 1179656 | tf_op jit(solution)/shard_map/ppermute | solution.py:20
  173.0 76.0 %copy-start.48 = (s32[1024]{0:T(1024)}, s32[1024]{0:T(1024)S(1)}, u32[]{:S(2)}) copy-start(s32[1024]{0:T(1024)S(1)} %get-tuple-element.109) | copy-start | bytes 12292
  192.5 9.4 %copy-start.38 = (s32[1,12]{1,0:T(1,128)S(1)}, s32[1,12]{1,0:T(1,128)}, u32[]{:S(2)}) copy-start(s32[1,12]{1,0:T(1,128)} %param.20) | copy-start | bytes 148
  196.7 9.8 %copy-start.6 = (bf16[256,768]{0,1:T(8,128)(2,1)S(1)}, bf16[256,768]{0,1:T(8,128)(2,1)}, u32[]{:S(2)}) copy-start(bf16[256,768]{0,1:T(8,128)(2,1)} %copy-done.5) | copy-start | bytes 1179652
  196.7 29.9 %collective-permute-start.2 = (bf16[3,1,196608]{2,0,1:T(4,128)(2,1)}, bf16[3,1,196608]{2,0,1:T(4,128)(2,1)}, u32[]{:S(2)}, u32[]{:S(2)}) collective-permute-start(bf16[3,1,196608]{2,0,1:T(4,128)(2,1)} %copy.147), channel_id=1, source_target_pairs={{0,1},{1,2},{2,3},{3,4},{4,5},{5,6},{6,7},{7,8},{8,9},{9,10},{10,1... | collective-permute-start | bytes 3538952 | tf_op jit(solution)/shard_map/ppermute | solution.py:17
  202.6 32.1 %collective-permute-start.3 = (bf16[3,1,196608]{2,0,1:T(4,128)(2,1)}, bf16[3,1,196608]{2,0,1:T(4,128)(2,1)}, u32[]{:S(2)}, u32[]{:S(2)}) collective-permute-start(bf16[3,1,196608]{2,0,1:T(4,128)(2,1)} %copy.147), channel_id=1, source_target_pairs={{1,0},{2,1},{3,2},{4,3},{5,4},{6,5},{7,6},{8,7},{9,8},{10,9},{11,1... | collective-permute-start | bytes 3538952 | tf_op jit(solution)/shard_map/ppermute | solution.py:20
  209.5 8.5 %copy-start.22 = (bf16[1,1,196608]{2,1,0:T(2,128)(2,1)S(1)}, bf16[1,1,196608]{2,1,0:T(2,128)(2,1)}, u32[]{:S(2)}) copy-start(bf16[1,1,196608]{2,1,0:T(2,128)(2,1)} %copy-done.21) | copy-start | bytes 1179652
  242.9 5.4 copy-start.46
  242.9 5.4 copy-start.67
  251.1 4.5 copy-start.41
  280.3 4.6 copy-start.2
  280.3 4.5 copy-start.4
  282.1 15.8 %collective-permute-start.4 = (bf16[1,1,196608]{2,0,1:T(2,128)(2,1)}, bf16[1,1,196608]{2,0,1:T(2,128)(2,1)S(1)}, u32[]{:S(2)}, u32[]{:S(2)}) collective-permute-start(bf16[1,1,196608]{2,0,1:T(2,128)(2,1)} %bitcast.34), channel_id=1, source_target_pairs={{0,64},{64,128},{128,192},{192,0},{1,65},{65,129},{129,193},{193,1... | collective-permute-start | bytes 1179656 | tf_op jit(solution)/shard_map/ppermute | solution.py:17
  282.1 15.8 %collective-permute-start.5 = (bf16[1,1,196608]{2,0,1:T(2,128)(2,1)}, bf16[1,1,196608]{2,0,1:T(2,128)(2,1)S(1)}, u32[]{:S(2)}, u32[]{:S(2)}) collective-permute-start(bf16[1,1,196608]{2,0,1:T(2,128)(2,1)} %bitcast.34), channel_id=1, source_target_pairs={{64,0},{128,64},{192,128},{0,192},{65,1},{129,65},{193,129},{1,193... | collective-permute-start | bytes 1179656 | tf_op jit(solution)/shard_map/ppermute | solution.py:20
  286.2 23.5 %copy-start.39 = (f32[1,64,128]{2,1,0:T(8,128)S(1)}, f32[1,64,128]{2,1,0:T(8,128)}, u32[]{:S(2)}) copy-start(f32[1,64,128]{2,1,0:T(8,128)} %convolution_bitcast_fusion.1) | copy-start | bytes 98308
  286.2 24.3 %copy-start.34 = (bf16[2,64,128]{2,1,0:T(8,128)(2,1)S(1)}, bf16[2,64,128]{2,1,0:T(8,128)(2,1)}, u32[]{:S(2)}) copy-start(bf16[2,64,128]{2,1,0:T(8,128)(2,1)} %param.15) | copy-start | bytes 98308
  297.9 5.0 copy-start.27
  297.9 4.9 copy-start.25
  302.8 268.8 %collective-permute-start.6 = (bf16[3,1,196608]{2,0,1:T(4,128)(2,1)}, bf16[3,1,196608]{2,0,1:T(4,128)(2,1)}, u32[]{:S(2)}, u32[]{:S(2)}) collective-permute-start(bf16[3,1,196608]{2,0,1:T(4,128)(2,1)} %pad_maximum_fusion.1), channel_id=1, source_target_pairs={{0,1},{1,2},{2,3},{3,4},{4,5},{5,6},{6,7},{7,8},{8,9},{9,10},{10,1... | collective-permute-start | bytes 3538952 | tf_op jit(solution)/shard_map/ppermute | solution.py:17
  310.5 269.2 %collective-permute-start.7 = (bf16[3,1,196608]{2,0,1:T(4,128)(2,1)}, bf16[3,1,196608]{2,0,1:T(4,128)(2,1)}, u32[]{:S(2)}, u32[]{:S(2)}) collective-permute-start(bf16[3,1,196608]{2,0,1:T(4,128)(2,1)} %pad_maximum_fusion.1), channel_id=1, source_target_pairs={{1,0},{2,1},{3,2},{4,3},{5,4},{6,5},{7,6},{8,7},{9,8},{10,9},{11,1... | collective-permute-start | bytes 3538952 | tf_op jit(solution)/shard_map/ppermute | solution.py:20
  552.6 10.5 %copy-start.26 = (bf16[1,1,196608]{2,0,1:T(2,128)(2,1)S(1)}, bf16[1,1,196608]{2,0,1:T(2,128)(2,1)}, u32[]{:S(2)}) copy-start(bf16[1,1,196608]{2,0,1:T(2,128)(2,1)} %copy-done.25) | copy-start | bytes 1179652
  593.3 13.5 %copy-start.47 = (pred[2]{0:T(512)(128)(4,1)S(1)}, pred[2]{0:T(512)(128)(4,1)}, u32[]{:S(2)}) copy-start(pred[2]{0:T(512)(128)(4,1)} %copy-done.44) | copy-start | bytes 10
  593.3 13.5 %copy-start.68 = (pred[2]{0:T(512)(128)(4,1)S(1)}, pred[2]{0:T(512)(128)(4,1)}, u32[]{:S(2)}) copy-start(pred[2]{0:T(512)(128)(4,1)} %get-tuple-element.89) | copy-start | bytes 10
  623.3 77.3 %copy-start.23 = (f32[256,12,64]{0,2,1:T(8,128)S(1)}, f32[256,12,64]{0,2,1:T(8,128)}, u32[]{:S(2)}) copy-start(f32[256,12,64]{0,2,1:T(8,128)} %convolution_add_fusion.3) | copy-start | bytes 2359300
  (42 other events, 98.4 us)
Sparse Core Ops, SparseCore 0:
  310.5 238.5 all-reduce.4
where the time goes:
time: 719 us; the launch traced here: 710 us
  waiting for transfers between devices  290 us (40%)
  local copies, waits for them, and re-layouts  146 us (20%)
  other arithmetic  109 us (15%)
  blocking collectives  75.1 us (10%)
  matrix products  43.3 us (6%)
  starting transfers between devices  30.4 us (4%)
  between operations  16.5 us (2%)
    psum x1, waiting for transfers between devices, local(): lax.psum((local_diff, local_conv, local_bias), ('region', 'dom'))  236 us
    psum x1, blocking collectives, local(): lax.psum((local_diff, local_conv, local_bias), ('region', 'dom'))  75.1 us
    scatter-add x24, other arithmetic, assign_slots(): return totals.at[bucket_slice].add(kept)  48.2 us
    select_n x24, local copies, waits for them, and re-layouts, assign_slots(): kept = jnp.where(live_slice[:, None, None], products, 0.0)  31.9 us
    slice x4, local copies, waits for them, and re-layouts, neighbour_stack(): rims[region_pos, dom_pos].reshape(block_count, block_rows, feat_width)  31.1 us
    ppermute x8, waiting for transfers between devices, from_behind(): return lax.ppermute(block, axis, route)  30 us
    gather x12, local copies, waits for them, and re-layouts, slot_products(): source_rows = jnp.take(sources, wanted, axis=0)  29 us
    ppermute x4, waiting for transfers between devices, padded(): lax.ppermute(lax.slice_in_dim(block, block.shape[dim] - width, None, axis...  24.2 us
  transfers between devices with their start and end apart: 17, of which 8 were waited for; matrix products, arithmetic and copies ran while one was open for 11% of the time, Pallas kernels for 0%

commit v1 on v0

v1 whole, which is shorter than its diff:
```python
import math

import jax
import jax.numpy as jnp
from jax import lax
from jax.experimental import pallas as pl
from jax.experimental.pallas import tpu as pltpu
from jax.sharding import PartitionSpec as P

BF16 = jnp.bfloat16
F32 = jnp.float32
CH = 64
PAIR = 2 * CH
BLK = 128
ROWS = 256
DIFF_ROWS = 128
BIAS_ROW = 224

VMEM = pl.BlockSpec(memory_space=pltpu.VMEM)
SMEM = pl.BlockSpec(memory_space=pltpu.SMEM)


def shift(block, axis, distance):
    count = lax.axis_size(axis)
    return lax.ppermute(block, axis, [(i, (i + distance) % count) for i in range(count)])


def call(body, outs, args, specs, flops, scratch=()):
    moved = sum(a.size * a.dtype.itemsize for a in args)
    moved += sum(math.prod(s) * jnp.dtype(d).itemsize for s, d in outs)
    return pl.pallas_call(
        body,
        out_shape=[jax.ShapeDtypeStruct(s, d) for s, d in outs],
        in_specs=specs,
        out_specs=[VMEM] * len(outs),
        scratch_shapes=list(scratch),
        compiler_params=pltpu.CompilerParams(vmem_limit_bytes=40 * 1024 * 1024),
        cost_estimate=pl.CostEstimate(flops=flops, bytes_accessed=moved, transcendentals=0),
    )(*args)


def dot(a, b):
    return jnp.dot(a, b, preferred_element_type=F32)


def dot_nt(a, b):
    return lax.dot_general(a, b, (((1,), (1,)), ((), ())), preferred_element_type=F32)


def dot_tn(a, b):
    return lax.dot_general(a, b, (((0,), (0,)), ((), ())), preferred_element_type=F32)


def place(rows, cols, offset_of):
    r = lax.broadcasted_iota(jnp.int32, (rows, cols), 0)
    c = lax.broadcasted_iota(jnp.int32, (rows, cols), 1)
    return jnp.where(c == offset_of(r), 1.0, 0.0).astype(BF16)


def low_lanes(shape):
    return lax.broadcasted_iota(jnp.int32, shape, 1) < CH


def half_turn(v):
    return pltpu.roll(v, CH, 1)


def conv_table(w0, w1):
    even = place(PAIR, 2 * PAIR, lambda r: jnp.where(r < CH, r, r + CH))
    odd = place(PAIR, 2 * PAIR, lambda r: jnp.where(r < CH, r + CH, r + PAIR))
    tap1_even = dot(w1, even)
    tap0_even = dot(w0, even)
    tap1_odd = dot(w1, odd)
    tap0_odd = dot(w0, odd)
    rows = [jnp.zeros_like(tap1_even), tap1_even, tap0_even + tap1_odd, tap0_odd]
    return jnp.concatenate(rows, axis=0).astype(BF16)


def diff_table(w):
    low = place(CH, PAIR, lambda r: r)
    high = place(CH, PAIR, lambda r: r + CH)
    return jnp.concatenate([dot(w, low), dot(w, high)], axis=0).astype(BF16)


def pairs(ref, j):
    return ref[:, j * PAIR : (j + 1) * PAIR]


def adjacency_body(source, target, count, tiles, adj, total):
    total[...] = jnp.zeros_like(total)

    def add_tile(e, carry):
        rows = pl.ds(pl.multiple_of(target[0, e] * BLK, BLK), BLK)
        s = source[0, e]
        total[s, rows, :] = total[s, rows, :] + tiles[e].astype(F32)
        return carry

    lax.fori_loop(0, count[0], add_tile, 0)
    for n in range(5):
        adj[n, :, :BLK] = total[2 * n].astype(BF16)
        adj[n, :, BLK:] = total[2 * n + 1].astype(BF16)


def gate_body(steps, x, cw, cb, gated, dfilt, dgate):
    table = conv_table(cw[0], cw[1])
    bias = cb[...]
    turned = half_turn(bias)
    low = low_lanes(bias.shape)
    bias_f = jnp.where(low, bias, turned)
    bias_g = jnp.where(low, turned, bias)
    for j in range(steps // 2):
        if j == 0:
            pre = dot(x[:, :PAIR], table[PAIR:])
        else:
            pre = dot(x[:, (j - 1) * PAIR : (j + 1) * PAIR], table)
        filt = jnp.tanh(pre[:, :PAIR] + bias_f)
        opened = jax.nn.sigmoid(pre[:, PAIR:] + bias_g)
        cols = slice(j * PAIR, (j + 1) * PAIR)
        both = filt * opened
        gated[:, cols] = both.astype(BF16)
        dfilt[:, cols] = opened * (1.0 - filt * filt)
        dgate[:, cols] = both * (1.0 - opened)


def first_body(adj, g, *outs):
    field = g[...]
    for n, out in zip((3, 4, 1, 2, 0), outs):
        out[...] = dot_tn(adj[n], field).astype(out.dtype)


def second_body(adj, own, p1, p2, p3, p4, u, *outs):
    total = own[...]
    for p in (p1, p2, p3, p4):
        total = total + p[...].astype(F32)
    field = total.astype(BF16)
    u[...] = field
    for n, out in zip((3, 4, 1, 2, 0), outs):
        out[...] = dot_tn(adj[n], field).astype(out.dtype)


def early_body(steps, g, u1, gated, dw, back, sums):
    t0 = diff_table(dw[0])
    t1 = diff_table(dw[1])
    acc = [jnp.zeros((PAIR, PAIR), F32) for _ in range(2)]
    for j in range(steps // 2):
        gj, uj, hj = pairs(g, j), pairs(u1, j), pairs(gated, j)
        back[:, j * PAIR : (j + 1) * PAIR] = dot_nt(gj, t0) + dot_nt(uj, t1)
        acc[0] = acc[0] + dot_tn(hj, gj)
        acc[1] = acc[1] + dot_tn(hj, uj)
    sums[0] = acc[0]
    sums[1] = acc[1]


def fold(q):
    return q[:CH] + half_turn(q[CH:])


def late_body(
    steps, x, gated, dfilt, dgate, own, p1, p2, p3, p4, back, sums, dw, dpre, partial
):
    t2 = diff_table(dw[2])
    half = steps // 2
    acc = jnp.zeros((PAIR, PAIR), F32)
    bias_f = jnp.zeros((1, PAIR), F32)
    bias_g = jnp.zeros((1, PAIR), F32)
    for j in range(half):
        cols = slice(j * PAIR, (j + 1) * PAIR)
        u2 = own[:, cols]
        for p in (p1, p2, p3, p4):
            u2 = u2 + p[:, cols].astype(F32)
        u2 = u2.astype(BF16)
        back_zero = back[:, cols] + dot_nt(u2, t2)
        df = (back_zero * dfilt[:, cols]).astype(BF16)
        dg = (back_zero * dgate[:, cols]).astype(BF16)
        dpre[:, 2 * j * PAIR : (2 * j + 1) * PAIR] = df
        dpre[:, (2 * j + 1) * PAIR : (2 * j + 2) * PAIR] = dg
        acc = acc + dot_tn(pairs(gated, j), u2)
        bias_f = bias_f + jnp.sum(df.astype(F32), axis=0, keepdims=True)
        bias_g = bias_g + jnp.sum(dg.astype(F32), axis=0, keepdims=True)
    here = jnp.zeros((PAIR, 2 * PAIR), F32)
    ahead = jnp.zeros((PAIR, 2 * PAIR), F32)
    for j in range(half):
        xj = pairs(x, j)
        if j + 1 < half:
            prod = dot_tn(xj, dpre[:, 2 * j * PAIR : (2 * j + 4) * PAIR])
            ahead = ahead + prod[:, 2 * PAIR :]
            here = here + prod[:, : 2 * PAIR]
        else:
            here = here + dot_tn(xj, dpre[:, 2 * j * PAIR : (2 * j + 2) * PAIR])
    low = low_lanes((CH, PAIR))
    top_f, top_g = here[:CH, :PAIR], here[:CH, PAIR:]
    bottom_f, bottom_g = here[CH:, :PAIR], here[CH:, PAIR:]
    next_f, next_g = ahead[CH:, :PAIR], ahead[CH:, PAIR:]
    partial[:CH] = jnp.where(low, top_f + half_turn(bottom_f), half_turn(top_g) + bottom_g)
    partial[CH:PAIR] = jnp.where(low, half_turn(top_f) + next_f, top_g + half_turn(next_g))
    q0, q1, q2 = fold(sums[0]), fold(sums[1]), fold(acc)
    partial[DIFF_ROWS : DIFF_ROWS + CH] = jnp.where(low, q0, half_turn(q1))
    partial[DIFF_ROWS + CH : BIAS_ROW] = jnp.where(low[:32], q2[:32], half_turn(q2[32:]))
    bias = jnp.where(
        low[:1], bias_f + half_turn(bias_f), bias_g + half_turn(bias_g)
    )
    row = lax.broadcasted_iota(jnp.int32, (ROWS - BIAS_ROW, PAIR), 0)
    partial[BIAS_ROW:] = jnp.where(row == 0, bias, 0.0)


def features_body(steps, g, dpre, cw, out):
    table = conv_table(cw[0], cw[1])
    here = table[PAIR:]
    ahead = table[:PAIR]
    half = steps // 2
    for j in range(half):
        cols = slice(j * PAIR, (j + 1) * PAIR)
        total = g[:, cols].astype(F32) + dot_nt(dpre[:, 2 * j * PAIR : (2 * j + 2) * PAIR], here)
        if j + 1 < half:
            total = total + dot_nt(dpre[:, (2 * j + 2) * PAIR : (2 * j + 4) * PAIR], ahead)
        out[:, cols] = total.astype(BF16)


def hop_body(adj, own, f1, f2, f3, f4, out):
    total = dot(adj[0], own[...])
    for n, f in ((1, f1), (2, f2), (3, f3), (4, f4)):
        total = total + dot(adj[n], f[...])
    out[...] = total.astype(BF16)


def mix_body(steps, adj, hop1, f1, f2, f3, f4, x, gated, dw, out):
    total = dot(adj[0], hop1[...])
    for n, f in ((1, f1), (2, f2), (3, f3), (4, f4)):
        total = total + dot(adj[n], f[...])
    hop2 = total.astype(BF16)
    t0, t1, t2 = diff_table(dw[0]), diff_table(dw[1]), diff_table(dw[2])
    for j in range(steps // 2):
        cols = slice(j * PAIR, (j + 1) * PAIR)
        mixed = x[:, cols].astype(F32) + dot(gated[:, cols], t0)
        mixed = mixed + dot(hop1[:, cols], t1) + dot(hop2[:, cols], t2)
        out[:, cols] = mixed.astype(BF16)


def finish_body(scale, full, diff, conv, bias):
    conv[0] = full[:CH] * scale
    conv[1] = full[CH:PAIR] * scale
    both = full[DIFF_ROWS : DIFF_ROWS + CH] * scale
    last = full[DIFF_ROWS + CH : BIAS_ROW] * scale
    diff[0] = both[:, :CH]
    diff[1] = half_turn(both)[:, :CH]
    diff[2, :32] = last[:, :CH]
    diff[2, 32:] = half_turn(last)[:, :CH]
    bias[...] = full[BIAS_ROW : BIAS_ROW + 1] * scale


def local(x, g, cw, cb, dw, tiles, source, target, count):
    cells, width = x.shape
    steps = width // CH
    both_axes = ("region", "dom")
    devices = lax.axis_size(both_axes)
    scale = 1.0 / math.sqrt(cells * devices * steps)
    field = ((cells, width), BF16)
    field32 = ((cells, width), F32)
    mac = 2 * cells * width

    (adj,) = call(
        adjacency_body,
        [((5, 2 * BLK, 2 * BLK), BF16)],
        (source, target, count, tiles),
        [SMEM, SMEM, SMEM, VMEM],
        0,
        [pltpu.VMEM((10, 2 * BLK, BLK), F32)],
    )

    def send_back(p3, p4, p1, p2):
        return (
            shift(p1, "dom", -1),
            shift(p2, "dom", 1),
            shift(p3, "region", -1),
            shift(p4, "region", 1),
        )

    def send_out(f):
        return (
            shift(f, "dom", 1),
            shift(f, "dom", -1),
            shift(f, "region", 1),
            shift(f, "region", -1),
        )

    *parts, own = call(
        first_body, [field] * 4 + [field32], (adj, g), [VMEM] * 2, mac * 5 * 2 * BLK
    )
    arrived = send_back(*parts)
    gated, dfilt, dgate = call(
        lambda *r: gate_body(steps, *r),
        [field, field32, field32],
        (x, cw, cb.reshape(1, -1)),
        [VMEM] * 3,
        mac * 2 * PAIR,
    )
    u1, *parts, own = call(
        second_body,
        [field] * 5 + [field32],
        (adj, own, *arrived),
        [VMEM] * 6,
        mac * 5 * 2 * BLK,
    )
    arrived = send_back(*parts)
    back, sums = call(
        lambda *r: early_body(steps, *r),
        [field32, ((2, PAIR, PAIR), F32)],
        (g, u1, gated, dw),
        [VMEM] * 4,
        mac * 4 * PAIR,
    )
    dpre, partial = call(
        lambda *r: late_body(steps, *r),
        [((cells, 2 * width), BF16), ((ROWS, PAIR), F32)],
        (x, gated, dfilt, dgate, own, *arrived, back, sums, dw),
        [VMEM] * 12,
        mac * 6 * PAIR,
    )
    spread = lax.all_to_all(partial, both_axes, 0, 0, tiled=True)
    piece = jnp.sum(spread, axis=0, keepdims=True)
    full = lax.all_to_all(
        jnp.broadcast_to(piece, (ROWS, PAIR)), both_axes, 0, 0, tiled=True
    )

    (grad_features,) = call(
        lambda *r: features_body(steps, *r),
        [field],
        (g, dpre, cw),
        [VMEM] * 3,
        mac * 4 * PAIR,
    )
    (hop1,) = call(
        hop_body, [field], (adj, gated, *send_out(gated)), [VMEM] * 6, mac * 5 * 2 * BLK
    )
    (mixed,) = call(
        lambda *r: mix_body(steps, *r),
        [field],
        (adj, hop1, *send_out(hop1), x, gated, dw),
        [VMEM] * 9,
        mac * 8 * 2 * BLK,
    )
    diff, conv, bias = call(
        lambda *r: finish_body(scale, *r),
        [((3, CH, CH), F32), ((2, CH, PAIR), F32), ((1, PAIR), F32)],
        (full,),
        [VMEM],
        0,
    )
    return mixed, grad_features, diff, conv, bias.reshape(-1)


def solution(mesh):
    split = P(("region", "dom"), None)
    in_specs = (
        split,
        split,
        P(),
        P(),
        P(),
        P(("region", "dom"), None, None),
        split,
        split,
        P(("region", "dom")),
    )
    out_specs = (split, split, P(), P(), P())
    return jax.shard_map(local, mesh=mesh, in_specs=in_specs, out_specs=out_specs, check_vma=False)
```

time: 719 us -> 88.2 us (0.12); the launches traced: 710 us -> 87.9 us
  waiting for transfers between devices: 290 us -> 25.6 us
  local copies, waits for them, and re-layouts: 146 us -> 4.26 us
  other arithmetic: 109 us -> 0.29 us
  blocking collectives: 75.1 us -> 0 us
  matrix products: 43.3 us -> 0 us
  between operations: 16.5 us -> 1.49 us
  starting transfers between devices: 30.4 us -> 43.4 us
  Pallas kernels: 0 us -> 12.8 us
    psum x1 -> x0, waiting for transfers between devices: 236 us -> none  [local(): lax.psum((local_diff, local_conv, local_bias), ('region', 'dom'))]
    psum x1 -> x0, blocking collectives: 75.1 us -> none  [local(): lax.psum((local_diff, local_conv, local_bias), ('region', 'dom'))]
    scatter-add x24 -> x0, other arithmetic: 48.2 us -> none  [assign_slots(): return totals.at[bucket_slice].add(kept)]
    dot_general x39 -> x0, matrix products: 43.3 us -> none  [the longest x12 17.1 us: slot_products(): jnp.einsum('sji,sjf->sif', tiles, own_rows, preferred_element_type=jnp.fl...]
    ppermute x16, waiting for transfers between devices: 54.2 us -> 13.4 us  [shift(): lax.ppermute(block, axis, [(i, (i + distance) % count) for i in range(cou...]
    gather x24 -> x0, local copies, waits for them, and re-layouts: 39.7 us -> none  [the longest x12 29 us: slot_products(): source_rows = jnp.take(sources, wanted, axis=0)]
    slice x6 -> x0, local copies, waits for them, and re-layouts: 36.7 us -> none  [the longest x4 31.1 us: neighbour_stack(): rims[region_pos, dom_pos].reshape(block_count, block_rows, feat_width)]
    ppermute x4 -> x0, other arithmetic: 32.6 us -> none  [the longest x2 16.3 us: padded(): lax.ppermute(lax.slice_in_dim(block, 0, width, axis=dim), axis, backward)]
  transfers between devices with their start and end apart: 17 -> 18, of which waited for: 8 -> 5; matrix products, arithmetic and copies ran while one was open for 11% -> 1% of each run, Pallas kernels for 0% -> 11%
where the time goes in v1:
time: 88.2 us; the launch traced here: 87.9 us
  starting transfers between devices  43.4 us (49%)
  waiting for transfers between devices  25.6 us (29%)
  Pallas kernels  12.8 us (15%)
  local copies, waits for them, and re-layouts  4.26 us (5%)
  between operations  1.49 us (2%)
    ppermute x16, starting transfers between devices, shift(): lax.ppermute(block, axis, [(i, (i + distance) % count) for i in range(cou...  26.9 us
    ppermute x16, waiting for transfers between devices, shift(): lax.ppermute(block, axis, [(i, (i + distance) % count) for i in range(cou...  13.4 us
    pallas_call x10, Pallas kernels, call(): pl.pallas_call(body, out_shape=[jax.ShapeDtypeStruct(s, d) for s, d in ou...  12.8 us
    all_to_all x1, starting transfers between devices, local(): lax.all_to_all(jnp.broadcast_to(piece, (ROWS, PAIR)), both_axes, 0, 0, ti...  9.64 us
    all_to_all x1, waiting for transfers between devices, local(): lax.all_to_all(jnp.broadcast_to(piece, (ROWS, PAIR)), both_axes, 0, 0, ti...  8.07 us
    all_to_all x1, starting transfers between devices, local(): spread = lax.all_to_all(partial, both_axes, 0, 0, tiled=True)  6.89 us
    all_to_all x1, waiting for transfers between devices, local(): spread = lax.all_to_all(partial, both_axes, 0, 0, tiled=True)  4.14 us
    unnamed x20, local copies, waits for them, and re-layouts  3.53 us
  transfers between devices with their start and end apart: 18, of which 5 were waited for; matrix products, arithmetic and copies ran while one was open for 1% of the time, Pallas kernels for 11%

profile of v1, /device:TPU:1, one launch (start us, length us, event | category | flops | bytes accessed | tf_op | source)
XLA Modules:
  0.0 87.9 jit_solution(10286548322220528350)
XLA Ops:
  0.6 0.0 copy-start.7
  0.6 0.0 copy-start.8
  1.3 0.0 copy-done.7
  1.3 0.0 copy-done.8
  1.3 0.0 copy-start.3
  1.3 1.0 %copy-done.3 = bf16[12,128,128]{2,1,0:T(8,128)(2,1)S(1)} copy-done((bf16[12,128,128]{2,1,0:T(8,128)(2,1)S(1)}, bf16[12,128,128]{2,1,0:T(8,128)(2,1)}, u32[]{:S(2)}) %copy-start.3) | copy-done | bytes 393240
  2.3 0.8 shard_map.128.adj.r_0_
  3.2 0.1 copy-done.1
  3.3 0.7 shard_map.132
  4.1 3.6 %collective-permute-start.10 = (bf16[256,768]{1,0:T(8,128)(2,1)S(1)}, bf16[256,768]{1,0:T(8,128)(2,1)S(1)}, u32[]{:S(2)}, u32[]{:S(2)}) collective-permute-start(bf16[256,768]{1,0:T(8,128)(2,1)S(1)} %get-tuple-element.32), channel_id=1, source_target_pairs={{0,192},{64,0},{128,64},{192,128},{1,193},{65,1},{129,65},{193,129... | collective-permute-start | bytes 1179656 | tf_op jit(solution)/shard_map/ppermute | solution.py:25
  7.7 0.0 collective-permute-start.11
  7.7 1.7 %collective-permute-start.8 = (bf16[256,768]{1,0:T(8,128)(2,1)S(1)}, bf16[256,768]{1,0:T(8,128)(2,1)S(1)}, u32[]{:S(2)}, u32[]{:S(2)}) collective-permute-start(bf16[256,768]{1,0:T(8,128)(2,1)S(1)} %get-tuple-element.30), channel_id=1, source_target_pairs={{0,63},{1,0},{2,1},{3,2},{4,3},{5,4},{6,5},{7,6},{8,7},{9,8},{10,9... | collective-permute-start | bytes 1179656 | tf_op jit(solution)/shard_map/ppermute | solution.py:25
  9.4 0.8 collective-permute-start.9
  10.2 5.3 %collective-permute-done.10.p3 = bf16[256,768]{1,0:T(8,128)(2,1)S(1)} collective-permute-done((bf16[256,768]{1,0:T(8,128)(2,1)S(1)}, bf16[256,768]{1,0:T(8,128)(2,1)S(1)}, u32[]{:S(2)}, u32[]{:S(2)}) %collective-permute-start.10) | collective-permute-done | bytes 393248 | tf_op jit(solution)/shard_map/ppermute | solution.py:25
  15.5 3.1 %collective-permute-done.11.p4 = bf16[256,768]{1,0:T(8,128)(2,1)S(1)} collective-permute-done((bf16[256,768]{1,0:T(8,128)(2,1)S(1)}, bf16[256,768]{1,0:T(8,128)(2,1)S(1)}, u32[]{:S(2)}, u32[]{:S(2)}) %collective-permute-start.11) | collective-permute-done | bytes 393248 | tf_op jit(solution)/shard_map/ppermute | solution.py:25
  18.6 0.0 collective-permute-done.8.p1
  18.6 0.0 collective-permute-done.9.p2
  18.6 0.0 copy-start.6
  18.6 0.9 shard_map.133
  19.5 7.9 %collective-permute-start.12 = (bf16[256,768]{1,0:T(8,128)(2,1)S(1)}, bf16[256,768]{1,0:T(8,128)(2,1)S(1)}, u32[]{:S(2)}, u32[]{:S(2)}) collective-permute-start(bf16[256,768]{1,0:T(8,128)(2,1)S(1)} %get-tuple-element.35), channel_id=1, source_target_pairs={{0,63},{1,0},{2,1},{3,2},{4,3},{5,4},{6,5},{7,6},{8,7},{9,8},{10,9... | collective-permute-start | bytes 1179656 | tf_op jit(solution)/shard_map/ppermute | solution.py:25
  27.3 0.0 collective-permute-start.13
  27.3 2.7 %collective-permute-start.14 = (bf16[256,768]{1,0:T(8,128)(2,1)S(1)}, bf16[256,768]{1,0:T(8,128)(2,1)S(1)}, u32[]{:S(2)}, u32[]{:S(2)}) collective-permute-start(bf16[256,768]{1,0:T(8,128)(2,1)S(1)} %get-tuple-element.37), channel_id=1, source_target_pairs={{0,192},{64,0},{128,64},{192,128},{1,193},{65,1},{129,65},{193,129... | collective-permute-start | bytes 1179656 | tf_op jit(solution)/shard_map/ppermute | solution.py:25
  30.0 0.0 collective-permute-start.15
  30.0 0.0 copy-done
  30.0 0.0 copy-done.6
  30.0 0.6 copy-done.9
  30.7 0.6 shard_map.129
  31.3 0.1 collective-permute-start
  31.4 0.0 collective-permute-done.12.r_5_
  31.4 1.6 %collective-permute-start.1 = (bf16[256,768]{1,0:T(8,128)(2,1)S(1)}, bf16[256,768]{1,0:T(8,128)(2,1)}, u32[]{:S(2)}, u32[]{:S(2)}) collective-permute-start(bf16[256,768]{1,0:T(8,128)(2,1)S(1)} %get-tuple-element.26.own.r_7_.r_2_.r_1_), channel_id=1, source_target_pairs={{0,63},{1,0},{2,1},{3,2},{4,3},{5,4},{6,5},{7,6},{8,7},{9,8},{10,9... | collective-permute-start | bytes 1179656 | tf_op jit(solution)/shard_map/ppermute | solution.py:25
  33.0 0.0 collective-permute-done.13.r_6_
  33.0 0.0 collective-permute-start.2
  33.0 5.0 %collective-permute-done.14.r_7_ = bf16[256,768]{1,0:T(8,128)(2,1)S(1)} collective-permute-done((bf16[256,768]{1,0:T(8,128)(2,1)S(1)}, bf16[256,768]{1,0:T(8,128)(2,1)S(1)}, u32[]{:S(2)}, u32[]{:S(2)}) %collective-permute-start.14) | collective-permute-done | bytes 393248 | tf_op jit(solution)/shard_map/ppermute | solution.py:25
  38.0 3.4 %collective-permute-start.3 = (bf16[256,768]{1,0:T(8,128)(2,1)S(1)}, bf16[256,768]{1,0:T(8,128)(2,1)}, u32[]{:S(2)}, u32[]{:S(2)}) collective-permute-start(bf16[256,768]{1,0:T(8,128)(2,1)S(1)} %get-tuple-element.26.own.r_7_.r_2_.r_1_), channel_id=1, source_target_pairs={{0,192},{64,0},{128,64},{192,128},{1,193},{65,1},{129,65},{193,129... | collective-permute-start | bytes 1179656 | tf_op jit(solution)/shard_map/ppermute | solution.py:25
  41.4 0.0 copy-done.2
  41.4 0.7 shard_map.134
  42.1 0.0 collective-permute-done.15.r_8_
  42.1 1.6 %shard_map.135 = (bf16[256,1536]{1,0:T(8,128)(2,1)S(1)}, f32[256,128]{1,0:T(8,128)}) custom-call(bf16[256,768]{1,0:T(8,128)(2,1)S(1)} %copy-done, bf16[256,768]{1,0:T(8,128)(2,1)S(1)} %get-tuple-element.26.own.r_7_.r_2_.r_1_, f32[256,768]{1,0:T(8,128)S(1)} %get-tuple-element.27.r_2_, f32[256,768]{1,0:T(8,128)S(1)} %get-tuple-element.28.r_3_, ...), custom_call_target="tpu_custom_call" | custom-call | flops 301989888 | bytes 6578176 | tf_op jit(solution)/shard_map/pallas_call | solution.py:31
  43.8 6.9 %all-to-all-start = ((f32[256,1,128]{2,1,0:T(1,128)}), f32[256,1,128]{2,1,0:T(1,128)S(1)}, u32[]{:S(2)}, u32[]{:S(2)}) async-start(f32[256,1,128]{2,1,0:T(1,128)} %bitcast.2), calls=%async_computation | async-start | bytes 262144 | tf_op jit(solution)/shard_map/all_to_all | solution.py:319
  50.7 0.0 collective-permute-done.f1
  50.7 0.0 copy-start.4
  50.7 0.7 copy-done.4
  51.4 0.0 collective-permute-done.1.f2
  51.4 0.0 collective-permute-done.2.f3
  51.4 0.0 collective-permute-done.3.f4
  51.4 0.0 copy-start.5
  51.5 1.0 %copy-done.5 = bf16[256,768]{1,0:T(8,128)(2,1)S(1)} copy-done((bf16[256,768]{1,0:T(8,128)(2,1)S(1)}, bf16[256,768]{1,0:T(8,128)(2,1)}, u32[]{:S(2)}) %copy-start.5) | copy-done | bytes 393240
  52.4 1.9 %shard_map.130.r_1_ = bf16[256,768]{1,0:T(8,128)(2,1)S(1)} custom-call(bf16[5,256,256]{2,1,0:T(8,128)(2,1)S(1)} %shard_map.128.adj.r_0_, bf16[256,768]{1,0:T(8,128)(2,1)S(1)} %get-tuple-element.26.own.r_7_.r_2_.r_1_, bf16[256,768]{1,0:T(8,128)(2,1)S(1)} %copy-done.5, bf16[256,768]{1,0:T(8,128)(2,1)} %collective-permute-done.1.f2, ...), custom_call_target="tpu_custom_call" | custom-call | flops 503316480 | bytes 3014656 | tf_op jit(solution)/shard_map/pallas_call | solution.py:31
  54.4 2.0 %collective-permute-start.4 = (bf16[256,768]{1,0:T(8,128)(2,1)S(1)}, bf16[256,768]{1,0:T(8,128)(2,1)}, u32[]{:S(2)}, u32[]{:S(2)}) collective-permute-start(bf16[256,768]{1,0:T(8,128)(2,1)S(1)} %shard_map.130.r_1_), channel_id=1, source_target_pairs={{0,1},{1,2},{2,3},{3,4},{4,5},{5,6},{6,7},{7,8},{8,9},{9,10},{10,1... | collective-permute-start | bytes 1179656 | tf_op jit(solution)/shard_map/ppermute | solution.py:25
  56.3 0.5 collective-permute-start.5
  56.8 0.8 collective-permute-start.6
  57.6 1.9 %collective-permute-start.7 = (bf16[256,768]{1,0:T(8,128)(2,1)S(1)}, bf16[256,768]{1,0:T(8,128)(2,1)}, u32[]{:S(2)}, u32[]{:S(2)}) collective-permute-start(bf16[256,768]{1,0:T(8,128)(2,1)S(1)} %shard_map.130.r_1_), channel_id=1, source_target_pairs={{0,192},{64,0},{128,64},{192,128},{1,193},{65,1},{129,65},{193,129... | collective-permute-start | bytes 1179656 | tf_op jit(solution)/shard_map/ppermute | solution.py:25
  59.5 4.1 %all-to-all-done = f32[256,1,128]{2,1,0:T(1,128)S(1)} async-done(((f32[256,1,128]{2,1,0:T(1,128)}), f32[256,1,128]{2,1,0:T(1,128)S(1)}, u32[]{:S(2)}, u32[]{:S(2)}) %all-to-all-start) | async-done | bytes 131104 | tf_op jit(solution)/shard_map/all_to_all | solution.py:319
  63.6 0.3 reduce_sum.9
  63.9 0.7 broadcast_in_dim.2
  64.6 9.6 %all-to-all-start.1 = ((f32[256,1,128]{2,1,0:T(1,128)}), f32[256,1,128]{2,1,0:T(1,128)S(1)}, u32[]{:S(2)}, u32[]{:S(2)}) async-start(f32[256,1,128]{2,1,0:T(1,128)} %broadcast_in_dim.2), calls=%async_computation.1 | async-start | bytes 262144 | tf_op jit(solution)/shard_map/all_to_all | solution.py:321
  74.3 1.4 %shard_map.136 = bf16[256,768]{1,0:T(8,128)(2,1)} custom-call(bf16[256,768]{1,0:T(8,128)(2,1)S(1)} %copy-done.1, bf16[256,1536]{1,0:T(8,128)(2,1)S(1)} %get-tuple-element.42.r_1_, bf16[2,64,128]{2,1,0:T(8,128)(2,1)S(1)} %copy-done.6), custom_call_target="tpu_custom_call" | custom-call | flops 201326592 | bytes 1605632 | tf_op jit(solution)/shard_map/pallas_call | solution.py:31
  75.8 0.0 collective-permute-done.4.r_2_
  75.8 0.0 collective-permute-done.5.r_3_
  75.8 0.0 collective-permute-done.6.r_4_
  75.8 0.0 collective-permute-done.7.r_5_
  75.8 3.3 %shard_map.131 = bf16[256,768]{1,0:T(8,128)(2,1)} custom-call(bf16[5,256,256]{2,1,0:T(8,128)(2,1)S(1)} %shard_map.128.adj.r_0_, bf16[256,768]{1,0:T(8,128)(2,1)S(1)} %shard_map.130.r_1_, bf16[256,768]{1,0:T(8,128)(2,1)} %collective-permute-done.4.r_2_, bf16[256,768]{1,0:T(8,128)(2,1)} %collective-permute-done.5.r_3_, ...), custom_call_target="tpu_custom_call" | custom-call | flops 805306368 | bytes 3825664 | tf_op jit(solution)/shard_map/pallas_call | solution.py:31
  79.1 8.1 %all-to-all-done.1 = f32[256,1,128]{2,1,0:T(1,128)S(1)} async-done(((f32[256,1,128]{2,1,0:T(1,128)}), f32[256,1,128]{2,1,0:T(1,128)S(1)}, u32[]{:S(2)}, u32[]{:S(2)}) %all-to-all-start.1) | async-done | bytes 131104 | tf_op jit(solution)/shard_map/all_to_all | solution.py:321
  87.2 0.7 shard_map.137
  (4 shorter events, 0.0 us)
Async XLA Ops:
  0.6 0.7 copy-start.7
  0.6 0.7 copy-start.8
  1.3 1.0 %copy-start.3 = (bf16[12,128,128]{2,1,0:T(8,128)(2,1)S(1)}, bf16[12,128,128]{2,1,0:T(8,128)(2,1)}, u32[]{:S(2)}) copy-start(bf16[12,128,128]{2,1,0:T(8,128)(2,1)} %tiles.1) | copy-start | bytes 1179652
  2.3 1.0 %copy-start.1 = (bf16[256,768]{1,0:T(8,128)(2,1)S(1)}, bf16[256,768]{1,0:T(8,128)(2,1)}, u32[]{:S(2)}) copy-start(bf16[256,768]{1,0:T(8,128)(2,1)} %r_0_.7) | copy-start | bytes 1179652
  4.1 11.4 %collective-permute-start.10 = (bf16[256,768]{1,0:T(8,128)(2,1)S(1)}, bf16[256,768]{1,0:T(8,128)(2,1)S(1)}, u32[]{:S(2)}, u32[]{:S(2)}) collective-permute-start(bf16[256,768]{1,0:T(8,128)(2,1)S(1)} %get-tuple-element.32), channel_id=1, source_target_pairs={{0,192},{64,0},{128,64},{192,128},{1,193},{65,1},{129,65},{193,129... | collective-permute-start | bytes 1179656 | tf_op jit(solution)/shard_map/ppermute | solution.py:25
  7.7 10.9 %collective-permute-start.11 = (bf16[256,768]{1,0:T(8,128)(2,1)S(1)}, bf16[256,768]{1,0:T(8,128)(2,1)S(1)}, u32[]{:S(2)}, u32[]{:S(2)}) collective-permute-start(bf16[256,768]{1,0:T(8,128)(2,1)S(1)} %get-tuple-element.33), channel_id=1, source_target_pairs={{0,64},{64,128},{128,192},{192,0},{1,65},{65,129},{129,193},{193,1... | collective-permute-start | bytes 1179656 | tf_op jit(solution)/shard_map/ppermute | solution.py:25
  7.7 10.9 %collective-permute-start.8 = (bf16[256,768]{1,0:T(8,128)(2,1)S(1)}, bf16[256,768]{1,0:T(8,128)(2,1)S(1)}, u32[]{:S(2)}, u32[]{:S(2)}) collective-permute-start(bf16[256,768]{1,0:T(8,128)(2,1)S(1)} %get-tuple-element.30), channel_id=1, source_target_pairs={{0,63},{1,0},{2,1},{3,2},{4,3},{5,4},{6,5},{7,6},{8,7},{9,8},{10,9... | collective-permute-start | bytes 1179656 | tf_op jit(solution)/shard_map/ppermute | solution.py:25
  9.4 9.2 %collective-permute-start.9 = (bf16[256,768]{1,0:T(8,128)(2,1)S(1)}, bf16[256,768]{1,0:T(8,128)(2,1)S(1)}, u32[]{:S(2)}, u32[]{:S(2)}) collective-permute-start(bf16[256,768]{1,0:T(8,128)(2,1)S(1)} %get-tuple-element.31), channel_id=1, source_target_pairs={{0,1},{1,2},{2,3},{3,4},{4,5},{5,6},{6,7},{7,8},{8,9},{9,10},{10,1... | collective-permute-start | bytes 1179656 | tf_op jit(solution)/shard_map/ppermute | solution.py:25
  18.6 11.5 %copy-start = (bf16[256,768]{1,0:T(8,128)(2,1)S(1)}, bf16[256,768]{1,0:T(8,128)(2,1)}, u32[]{:S(2)}) copy-start(bf16[256,768]{1,0:T(8,128)(2,1)} %r_0_.6) | copy-start | bytes 1179652
  18.6 11.5 %copy-start.6 = (bf16[2,64,128]{2,1,0:T(8,128)(2,1)S(1)}, bf16[2,64,128]{2,1,0:T(8,128)(2,1)}, u32[]{:S(2)}) copy-start(bf16[2,64,128]{2,1,0:T(8,128)(2,1)} %r_2_.1) | copy-start | bytes 98308
  19.5 12.0 %collective-permute-start.12 = (bf16[256,768]{1,0:T(8,128)(2,1)S(1)}, bf16[256,768]{1,0:T(8,128)(2,1)S(1)}, u32[]{:S(2)}, u32[]{:S(2)}) collective-permute-start(bf16[256,768]{1,0:T(8,128)(2,1)S(1)} %get-tuple-element.35), channel_id=1, source_target_pairs={{0,63},{1,0},{2,1},{3,2},{4,3},{5,4},{6,5},{7,6},{8,7},{9,8},{10,9... | collective-permute-start | bytes 1179656 | tf_op jit(solution)/shard_map/ppermute | solution.py:25
  27.3 5.7 %collective-permute-start.13 = (bf16[256,768]{1,0:T(8,128)(2,1)S(1)}, bf16[256,768]{1,0:T(8,128)(2,1)S(1)}, u32[]{:S(2)}, u32[]{:S(2)}) collective-permute-start(bf16[256,768]{1,0:T(8,128)(2,1)S(1)} %get-tuple-element.36), channel_id=1, source_target_pairs={{0,1},{1,2},{2,3},{3,4},{4,5},{5,6},{6,7},{7,8},{8,9},{9,10},{10,1... | collective-permute-start | bytes 1179656 | tf_op jit(solution)/shard_map/ppermute | solution.py:25
  27.3 10.6 %collective-permute-start.14 = (bf16[256,768]{1,0:T(8,128)(2,1)S(1)}, bf16[256,768]{1,0:T(8,128)(2,1)S(1)}, u32[]{:S(2)}, u32[]{:S(2)}) collective-permute-start(bf16[256,768]{1,0:T(8,128)(2,1)S(1)} %get-tuple-element.37), channel_id=1, source_target_pairs={{0,192},{64,0},{128,64},{192,128},{1,193},{65,1},{129,65},{193,129... | collective-permute-start | bytes 1179656 | tf_op jit(solution)/shard_map/ppermute | solution.py:25
  30.0 0.7 copy-start.9
  30.0 12.1 %collective-permute-start.15 = (bf16[256,768]{1,0:T(8,128)(2,1)S(1)}, bf16[256,768]{1,0:T(8,128)(2,1)S(1)}, u32[]{:S(2)}, u32[]{:S(2)}) collective-permute-start(bf16[256,768]{1,0:T(8,128)(2,1)S(1)} %get-tuple-element.38), channel_id=1, source_target_pairs={{0,64},{64,128},{128,192},{192,0},{1,65},{65,129},{129,193},{193,1... | collective-permute-start | bytes 1179656 | tf_op jit(solution)/shard_map/ppermute | solution.py:25
  30.7 10.7 %copy-start.2 = (bf16[3,64,64]{2,1,0:T(8,128)(2,1)S(1)}, bf16[3,64,64]{2,1,0:T(8,128)(2,1)}, u32[]{:S(2)}) copy-start(bf16[3,64,64]{2,1,0:T(8,128)(2,1)} %r_11_.1) | copy-start | bytes 73732
  31.3 19.3 %collective-permute-start = (bf16[256,768]{1,0:T(8,128)(2,1)S(1)}, bf16[256,768]{1,0:T(8,128)(2,1)S(1)}, u32[]{:S(2)}, u32[]{:S(2)}) collective-permute-start(bf16[256,768]{1,0:T(8,128)(2,1)S(1)} %get-tuple-element.26.own.r_7_.r_2_.r_1_), channel_id=1, source_target_pairs={{0,1},{1,2},{2,3},{3,4},{4,5},{5,6},{6,7},{7,8},{8,9},{9,10},{10,1... | collective-permute-start | bytes 1179656 | tf_op jit(solution)/shard_map/ppermute | solution.py:25
  31.4 20.0 %collective-permute-start.1 = (bf16[256,768]{1,0:T(8,128)(2,1)S(1)}, bf16[256,768]{1,0:T(8,128)(2,1)}, u32[]{:S(2)}, u32[]{:S(2)}) collective-permute-start(bf16[256,768]{1,0:T(8,128)(2,1)S(1)} %get-tuple-element.26.own.r_7_.r_2_.r_1_), channel_id=1, source_target_pairs={{0,63},{1,0},{2,1},{3,2},{4,3},{5,4},{6,5},{7,6},{8,7},{9,8},{10,9... | collective-permute-start | bytes 1179656 | tf_op jit(solution)/shard_map/ppermute | solution.py:25
  33.0 18.4 %collective-permute-start.2 = (bf16[256,768]{1,0:T(8,128)(2,1)S(1)}, bf16[256,768]{1,0:T(8,128)(2,1)}, u32[]{:S(2)}, u32[]{:S(2)}) collective-permute-start(bf16[256,768]{1,0:T(8,128)(2,1)S(1)} %get-tuple-element.26.own.r_7_.r_2_.r_1_), channel_id=1, source_target_pairs={{0,64},{64,128},{128,192},{192,0},{1,65},{65,129},{129,193},{193,1... | collective-permute-start | bytes 1179656 | tf_op jit(solution)/shard_map/ppermute | solution.py:25
  38.0 13.5 %collective-permute-start.3 = (bf16[256,768]{1,0:T(8,128)(2,1)S(1)}, bf16[256,768]{1,0:T(8,128)(2,1)}, u32[]{:S(2)}, u32[]{:S(2)}) collective-permute-start(bf16[256,768]{1,0:T(8,128)(2,1)S(1)} %get-tuple-element.26.own.r_7_.r_2_.r_1_), channel_id=1, source_target_pairs={{0,192},{64,0},{128,64},{192,128},{1,193},{65,1},{129,65},{193,129... | collective-permute-start | bytes 1179656 | tf_op jit(solution)/shard_map/ppermute | solution.py:25
  43.8 19.9 %all-to-all-start = ((f32[256,1,128]{2,1,0:T(1,128)}), f32[256,1,128]{2,1,0:T(1,128)S(1)}, u32[]{:S(2)}, u32[]{:S(2)}) async-start(f32[256,1,128]{2,1,0:T(1,128)} %bitcast.2), calls=%async_computation | async-start | bytes 262144 | tf_op jit(solution)/shard_map/all_to_all | solution.py:319
  50.7 0.7 copy-start.4
  51.4 1.0 %copy-start.5 = (bf16[256,768]{1,0:T(8,128)(2,1)S(1)}, bf16[256,768]{1,0:T(8,128)(2,1)}, u32[]{:S(2)}) copy-start(bf16[256,768]{1,0:T(8,128)(2,1)} %copy-done.4) | copy-start | bytes 1179652
  54.4 21.4 %collective-permute-start.4 = (bf16[256,768]{1,0:T(8,128)(2,1)S(1)}, bf16[256,768]{1,0:T(8,128)(2,1)}, u32[]{:S(2)}, u32[]{:S(2)}) collective-permute-start(bf16[256,768]{1,0:T(8,128)(2,1)S(1)} %shard_map.130.r_1_), channel_id=1, source_target_pairs={{0,1},{1,2},{2,3},{3,4},{4,5},{5,6},{6,7},{7,8},{8,9},{9,10},{10,1... | collective-permute-start | bytes 1179656 | tf_op jit(solution)/shard_map/ppermute | solution.py:25
  56.3 19.4 %collective-permute-start.5 = (bf16[256,768]{1,0:T(8,128)(2,1)S(1)}, bf16[256,768]{1,0:T(8,128)(2,1)}, u32[]{:S(2)}, u32[]{:S(2)}) collective-permute-start(bf16[256,768]{1,0:T(8,128)(2,1)S(1)} %shard_map.130.r_1_), channel_id=1, source_target_pairs={{0,63},{1,0},{2,1},{3,2},{4,3},{5,4},{6,5},{7,6},{8,7},{9,8},{10,9... | collective-permute-start | bytes 1179656 | tf_op jit(solution)/shard_map/ppermute | solution.py:25
  56.8 18.9 %collective-permute-start.6 = (bf16[256,768]{1,0:T(8,128)(2,1)S(1)}, bf16[256,768]{1,0:T(8,128)(2,1)}, u32[]{:S(2)}, u32[]{:S(2)}) collective-permute-start(bf16[256,768]{1,0:T(8,128)(2,1)S(1)} %shard_map.130.r_1_), channel_id=1, source_target_pairs={{0,64},{64,128},{128,192},{192,0},{1,65},{65,129},{129,193},{193,1... | collective-permute-start | bytes 1179656 | tf_op jit(solution)/shard_map/ppermute | solution.py:25
  57.6 18.2 %collective-permute-start.7 = (bf16[256,768]{1,0:T(8,128)(2,1)S(1)}, bf16[256,768]{1,0:T(8,128)(2,1)}, u32[]{:S(2)}, u32[]{:S(2)}) collective-permute-start(bf16[256,768]{1,0:T(8,128)(2,1)S(1)} %shard_map.130.r_1_), channel_id=1, source_target_pairs={{0,192},{64,0},{128,64},{192,128},{1,193},{65,1},{129,65},{193,129... | collective-permute-start | bytes 1179656 | tf_op jit(solution)/shard_map/ppermute | solution.py:25
  64.6 22.5 %all-to-all-start.1 = ((f32[256,1,128]{2,1,0:T(1,128)}), f32[256,1,128]{2,1,0:T(1,128)S(1)}, u32[]{:S(2)}, u32[]{:S(2)}) async-start(f32[256,1,128]{2,1,0:T(1,128)} %broadcast_in_dim.2), calls=%async_computation.1 | async-start | bytes 262144 | tf_op jit(solution)/shard_map/all_to_all | solution.py:321

commit v2 on v1

--- a/solution.py
+++ b/solution.py
@@ -20,9 +20,27 @@
 SMEM = pl.BlockSpec(memory_space=pltpu.SMEM)
 
 
-def shift(block, axis, distance):
+DOM = ("x", "z", "c")
+ALL = ("r", "x", "z", "c")
+
+
+def swap(block, axis, first):
     count = lax.axis_size(axis)
-    return lax.ppermute(block, axis, [(i, (i + distance) % count) for i in range(count)])
+    route = []
+    for i in range(count):
+        step = 1 if i % 2 == first else -1
+        route.append((i, (i + step) % count))
+    return lax.ppermute(block, axis, route)
+
+
+def trade(blocks):
+    core, cross, even, odd = blocks
+    return (
+        swap(core, DOM, 0),
+        swap(cross, DOM, 1),
+        swap(even, "r", 0),
+        swap(odd, "r", 1),
+    )
 
 
 def call(body, outs, args, specs, flops, scratch=()):
@@ -34,7 +52,7 @@
         in_specs=specs,
         out_specs=[VMEM] * len(outs),
         scratch_shapes=list(scratch),
-        compiler_params=pltpu.CompilerParams(vmem_limit_bytes=40 * 1024 * 1024),
+        compiler_params=pltpu.CompilerParams(vmem_limit_bytes=16 * 1024 * 1024),
         cost_estimate=pl.CostEstimate(flops=flops, bytes_accessed=moved, transcendentals=0),
     )(*args)
 
@@ -88,10 +106,17 @@
 
 def adjacency_body(source, target, count, tiles, adj, total):
     total[...] = jnp.zeros_like(total)
+    odd_core = lax.axis_index("c")
+    odd_region = lax.rem(lax.axis_index("r"), 2)
 
     def add_tile(e, carry):
         rows = pl.ds(pl.multiple_of(target[0, e] * BLK, BLK), BLK)
         s = source[0, e]
+        choice = lax.shift_right_logical(s, 1)
+        dom_trade = jnp.where(choice == 2 - odd_core, 1, 2)
+        region_trade = jnp.where(choice == 4 - odd_region, 3, 4)
+        met = jnp.where(choice == 0, 0, jnp.where(choice < 3, dom_trade, region_trade))
+        s = 2 * met + lax.bitwise_and(s, 1)
         total[s, rows, :] = total[s, rows, :] + tiles[e].astype(F32)
         return carry
 
@@ -124,7 +149,7 @@
 
 def first_body(adj, g, *outs):
     field = g[...]
-    for n, out in zip((3, 4, 1, 2, 0), outs):
+    for n, out in zip((1, 2, 3, 4, 0), outs):
         out[...] = dot_tn(adj[n], field).astype(out.dtype)
 
 
@@ -134,7 +159,7 @@
         total = total + p[...].astype(F32)
     field = total.astype(BF16)
     u[...] = field
-    for n, out in zip((3, 4, 1, 2, 0), outs):
+    for n, out in zip((1, 2, 3, 4, 0), outs):
         out[...] = dot_tn(adj[n], field).astype(out.dtype)
 
 
@@ -251,8 +276,7 @@
 def local(x, g, cw, cb, dw, tiles, source, target, count):
     cells, width = x.shape
     steps = width // CH
-    both_axes = ("region", "dom")
-    devices = lax.axis_size(both_axes)
+    devices = lax.axis_size(ALL)
     scale = 1.0 / math.sqrt(cells * devices * steps)
     field = ((cells, width), BF16)
     field32 = ((cells, width), F32)
@@ -267,26 +291,10 @@
         [pltpu.VMEM((10, 2 * BLK, BLK), F32)],
     )
 
-    def send_back(p3, p4, p1, p2):
-        return (
-            shift(p1, "dom", -1),
-            shift(p2, "dom", 1),
-            shift(p3, "region", -1),
-            shift(p4, "region", 1),
-        )
-
-    def send_out(f):
-        return (
-            shift(f, "dom", 1),
-            shift(f, "dom", -1),
-            shift(f, "region", 1),
-            shift(f, "region", -1),
-        )
-
     *parts, own = call(
         first_body, [field] * 4 + [field32], (adj, g), [VMEM] * 2, mac * 5 * 2 * BLK
     )
-    arrived = send_back(*parts)
+    arrived = trade(parts)
     gated, dfilt, dgate = call(
         lambda *r: gate_body(steps, *r),
         [field, field32, field32],
@@ -301,7 +309,7 @@
         [VMEM] * 6,
         mac * 5 * 2 * BLK,
     )
-    arrived = send_back(*parts)
+    arrived = trade(parts)
     back, sums = call(
         lambda *r: early_body(steps, *r),
         [field32, ((2, PAIR, PAIR), F32)],
@@ -316,11 +324,14 @@
         [VMEM] * 12,
         mac * 6 * PAIR,
     )
-    spread = lax.all_to_all(partial, both_axes, 0, 0, tiled=True)
-    piece = jnp.sum(spread, axis=0, keepdims=True)
-    full = lax.all_to_all(
-        jnp.broadcast_to(piece, (ROWS, PAIR)), both_axes, 0, 0, tiled=True
-    )
+    plane, depth = ("r", "x", "c"), lax.axis_size("z")
+    width_p = lax.axis_size(plane)
+    rows = ROWS // width_p
+    piece = lax.all_to_all(partial.reshape(width_p, rows, PAIR), plane, 0, 0, tiled=True)
+    piece = jnp.broadcast_to(jnp.sum(piece, axis=0), (depth, rows, PAIR))
+    piece = jnp.sum(lax.all_to_all(piece, "z", 0, 0, tiled=True), axis=0)
+    piece = jnp.broadcast_to(piece, (width_p, rows, PAIR))
+    full = lax.all_to_all(piece, plane, 0, 0, tiled=True).reshape(ROWS, PAIR)
 
     (grad_features,) = call(
         lambda *r: features_body(steps, *r),
@@ -330,12 +341,12 @@
         mac * 4 * PAIR,
     )
     (hop1,) = call(
-        hop_body, [field], (adj, gated, *send_out(gated)), [VMEM] * 6, mac * 5 * 2 * BLK
+        hop_body, [field], (adj, gated, *trade([gated] * 4)), [VMEM] * 6, mac * 5 * 2 * BLK
     )
     (mixed,) = call(
         lambda *r: mix_body(steps, *r),
         [field],
-        (adj, hop1, *send_out(hop1), x, gated, dw),
+        (adj, hop1, *trade([hop1] * 4), x, gated, dw),
         [VMEM] * 9,
         mac * 8 * 2 * BLK,
     )
@@ -350,17 +361,15 @@
 
 
 def solution(mesh):
-    split = P(("region", "dom"), None)
-    in_specs = (
-        split,
-        split,
-        P(),
-        P(),
-        P(),
-        P(("region", "dom"), None, None),
-        split,
-        split,
-        P(("region", "dom")),
-    )
+    region, dom = mesh.devices.shape
+    grid = mesh.devices.reshape(region, dom // 16, 8, 2)
+    split = P(ALL, None)
+    in_specs = (split, split, P(), P(), P(), P(ALL, None, None), split, split, P(ALL))
     out_specs = (split, split, P(), P(), P())
-    return jax.shard_map(local, mesh=mesh, in_specs=in_specs, out_specs=out_specs, check_vma=False)
+    return jax.shard_map(
+        local,
+        mesh=jax.sharding.Mesh(grid, ALL),
+        in_specs=in_specs,
+        out_specs=out_specs,
+        check_vma=False,
+    )

time: 88.2 us -> 85 us (0.964)
  blocking collectives: 0 us -> 28.6 us
  waiting for transfers between devices: 25.6 us -> 3 us
  starting transfers between devices: 43.4 us -> 38.8 us
  local copies, waits for them, and re-layouts: 4.26 us -> 1.87 us
  Pallas kernels: 12.8 us -> 10.9 us
    all_to_all x0 -> x2, blocking collectives: none -> 28.6 us  [the longest x1 16.6 us: local(): lax.all_to_all(partial.reshape(width_p, rows, PAIR), plane, 0, 0, tiled=T...]
    ppermute x16, waiting for transfers between devices: 13.4 us -> 0.04 us  [swap(): return lax.ppermute(block, axis, route)]
    all_to_all x2 -> x1, starting transfers between devices: 16.5 us -> 5.23 us  [local(): full = lax.all_to_all(piece, plane, 0, 0, tiled=True).reshape(ROWS, PAIR)]
    all_to_all x2 -> x1, waiting for transfers between devices: 12.2 us -> 2.95 us  [local(): full = lax.all_to_all(piece, plane, 0, 0, tiled=True).reshape(ROWS, PAIR)]
    ppermute x16, starting transfers between devices: 26.9 us -> 33.6 us  [swap(): return lax.ppermute(block, axis, route)]
    unnamed x20 -> x16, local copies, waits for them, and re-layouts: 3.53 us -> 1.21 us
    pallas_call x10, Pallas kernels: 12.8 us -> 10.9 us  [call(): pl.pallas_call(body, out_shape=[jax.ShapeDtypeStruct(s, d) for s, d in ou...]
  transfers between devices with their start and end apart: 18 -> 17, of which waited for: 5 -> 1; matrix products, arithmetic and copies ran while one was open for 1% -> 1% of each run, Pallas kernels for 11% -> 10%
where the time goes in v2:
time: 85 us; the launch traced here: 84.7 us
  starting transfers between devices  38.8 us (46%)
  blocking collectives  28.6 us (34%)
  Pallas kernels  10.9 us (13%)
  waiting for transfers between devices  3 us (4%)
  local copies, waits for them, and re-layouts  1.87 us (2%)
  between operations  1.45 us (2%)
    ppermute x16, starting transfers between devices, swap(): return lax.ppermute(block, axis, route)  33.6 us
    all_to_all x1, blocking collectives, local(): lax.all_to_all(partial.reshape(width_p, rows, PAIR), plane, 0, 0, tiled=T...  16.6 us
    all_to_all x1, blocking collectives, local(): piece = jnp.sum(lax.all_to_all(piece, 'z', 0, 0, tiled=True), axis=0)  12 us
    pallas_call x10, Pallas kernels, call(): pl.pallas_call(body, out_shape=[jax.ShapeDtypeStruct(s, d) for s, d in ou...  10.9 us
    all_to_all x1, starting transfers between devices, local(): full = lax.all_to_all(piece, plane, 0, 0, tiled=True).reshape(ROWS, PAIR)  5.23 us
    all_to_all x1, waiting for transfers between devices, local(): full = lax.all_to_all(piece, plane, 0, 0, tiled=True).reshape(ROWS, PAIR)  2.95 us
  transfers between devices with their start and end apart: 17, of which 1 were waited for; matrix products, arithmetic and copies ran while one was open for 1% of the time, Pallas kernels for 10%

profile of v2, /device:TPU:1, one launch (start us, length us, event | category | flops | bytes accessed | tf_op | source)
XLA Modules:
  0.0 84.7 jit_solution(13659495439046494822)
XLA Ops:
  0.6 0.0 copy-start.5
  0.6 0.0 copy-start.6
  1.3 0.0 copy-done.5
  1.3 0.0 copy-done.6
  1.3 0.0 copy-start.3
  1.3 1.0 %copy-done.3 = bf16[12,128,128]{2,1,0:T(8,128)(2,1)S(1)} copy-done((bf16[12,128,128]{2,1,0:T(8,128)(2,1)S(1)}, bf16[12,128,128]{2,1,0:T(8,128)(2,1)}, u32[]{:S(2)}) %copy-start.3) | copy-done | bytes 393240
  2.3 0.0 copy-start.1
  2.3 0.8 shard_map.128.adj.r_0_
  3.1 0.2 copy-done.1
  3.3 0.0 copy-start
  3.3 0.0 copy-start.4
  3.3 0.7 shard_map.132
  4.1 2.2 %collective-permute-start.10 = (bf16[256,768]{1,0:T(8,128)(2,1)S(1)}, bf16[256,768]{1,0:T(8,128)(2,1)S(1)}, u32[]{:S(2)}, u32[]{:S(2)}) collective-permute-start(bf16[256,768]{1,0:T(8,128)(2,1)S(1)} %get-tuple-element.32), channel_id=1, source_target_pairs={{0,64},{64,0},{128,192},{192,128},{1,65},{65,1},{129,193},{193,129... | collective-permute-start | bytes 1179656 | tf_op jit(solution)/shard_map/ppermute | solution.py:33
  6.3 1.9 %collective-permute-start.11 = (bf16[256,768]{1,0:T(8,128)(2,1)S(1)}, bf16[256,768]{1,0:T(8,128)(2,1)S(1)}, u32[]{:S(2)}, u32[]{:S(2)}) collective-permute-start(bf16[256,768]{1,0:T(8,128)(2,1)S(1)} %get-tuple-element.33), channel_id=1, source_target_pairs={{0,192},{64,128},{128,64},{192,0},{1,193},{65,129},{129,65},{193,1... | collective-permute-start | bytes 1179656 | tf_op jit(solution)/shard_map/ppermute | solution.py:33
  8.2 1.2 %collective-permute-start.8 = (bf16[256,768]{1,0:T(8,128)(2,1)S(1)}, bf16[256,768]{1,0:T(8,128)(2,1)S(1)}, u32[]{:S(2)}, u32[]{:S(2)}) collective-permute-start(bf16[256,768]{1,0:T(8,128)(2,1)S(1)} %get-tuple-element.30), channel_id=1, source_target_pairs={{0,1},{1,0},{2,3},{3,2},{4,5},{5,4},{6,7},{7,6},{8,9},{9,8},{10,11... | collective-permute-start | bytes 1179656 | tf_op jit(solution)/shard_map/ppermute | solution.py:33
  9.4 0.0 copy-start.7
  9.4 1.5 %collective-permute-start.9 = (bf16[256,768]{1,0:T(8,128)(2,1)S(1)}, bf16[256,768]{1,0:T(8,128)(2,1)S(1)}, u32[]{:S(2)}, u32[]{:S(2)}) collective-permute-start(bf16[256,768]{1,0:T(8,128)(2,1)S(1)} %get-tuple-element.31), channel_id=1, source_target_pairs={{0,63},{1,2},{2,1},{3,4},{4,3},{5,6},{6,5},{7,8},{8,7},{9,10},{10,... | collective-permute-start | bytes 1179656 | tf_op jit(solution)/shard_map/ppermute | solution.py:33
  10.9 0.0 copy-done
  10.9 0.0 copy-done.4
  10.9 0.0 copy-done.7
  10.9 0.6 shard_map.129
  11.6 6.7 %collective-permute-start = (bf16[256,768]{1,0:T(8,128)(2,1)S(1)}, bf16[256,768]{1,0:T(8,128)(2,1)S(1)}, u32[]{:S(2)}, u32[]{:S(2)}) collective-permute-start(bf16[256,768]{1,0:T(8,128)(2,1)S(1)} %get-tuple-element.26.own.r_7_.r_2_.r_1_), channel_id=1, source_target_pairs={{0,1},{1,0},{2,3},{3,2},{4,5},{5,4},{6,7},{7,6},{8,9},{9,8},{10,11... | collective-permute-start | bytes 1179656 | tf_op jit(solution)/shard_map/ppermute | solution.py:33
  18.3 0.0 collective-permute-done.10.p3
  18.3 0.0 collective-permute-start.1
  18.3 0.0 collective-permute-done.11.p4
  18.3 1.0 %collective-permute-start.2 = (bf16[256,768]{1,0:T(8,128)(2,1)S(1)}, bf16[256,768]{1,0:T(8,128)(2,1)S(1)}, u32[]{:S(2)}, u32[]{:S(2)}) collective-permute-start(bf16[256,768]{1,0:T(8,128)(2,1)S(1)} %get-tuple-element.26.own.r_7_.r_2_.r_1_), channel_id=1, source_target_pairs={{0,64},{64,0},{128,192},{192,128},{1,65},{65,1},{129,193},{193,129... | collective-permute-start | bytes 1179656 | tf_op jit(solution)/shard_map/ppermute | solution.py:33
  19.3 0.0 collective-permute-done.8.p1
  19.3 1.9 %collective-permute-start.3 = (bf16[256,768]{1,0:T(8,128)(2,1)S(1)}, bf16[256,768]{1,0:T(8,128)(2,1)S(1)}, u32[]{:S(2)}, u32[]{:S(2)}) collective-permute-start(bf16[256,768]{1,0:T(8,128)(2,1)S(1)} %get-tuple-element.26.own.r_7_.r_2_.r_1_), channel_id=1, source_target_pairs={{0,192},{64,128},{128,64},{192,0},{1,193},{65,129},{129,65},{193,1... | collective-permute-start | bytes 1179656 | tf_op jit(solution)/shard_map/ppermute | solution.py:33
  21.2 0.0 collective-permute-done.9.p2
  21.2 0.9 %shard_map.133 = (bf16[256,768]{1,0:T(8,128)(2,1)S(1)}, bf16[256,768]{1,0:T(8,128)(2,1)S(1)}, bf16[256,768]{1,0:T(8,128)(2,1)S(1)}, bf16[256,768]{1,0:T(8,128)(2...) custom-call(bf16[5,256,256]{2,1,0:T(8,128)(2,1)S(1)} %shard_map.128.adj.r_0_, ...), custom_call_target="tpu_custom_call" | custom-call | flops 503316480 | bytes 5767168 | tf_op jit(solution)/shard_map/pallas_call | solution.py:49
  22.1 5.7 %collective-permute-start.12 = (bf16[256,768]{1,0:T(8,128)(2,1)S(1)}, bf16[256,768]{1,0:T(8,128)(2,1)S(1)}, u32[]{:S(2)}, u32[]{:S(2)}) collective-permute-start(bf16[256,768]{1,0:T(8,128)(2,1)S(1)} %get-tuple-element.35), channel_id=1, source_target_pairs={{0,1},{1,0},{2,3},{3,2},{4,5},{5,4},{6,7},{7,6},{8,9},{9,8},{10,11... | collective-permute-start | bytes 1179656 | tf_op jit(solution)/shard_map/ppermute | solution.py:33
  27.9 0.0 collective-permute-done.f1
  27.9 0.0 collective-permute-start.13
  27.9 0.0 collective-permute-done.1.f2
  27.9 0.5 collective-permute-start.14
  28.4 0.0 collective-permute-done.2.f3
  28.4 0.0 copy-start.2
  28.4 0.5 collective-permute-start.15
  28.8 0.0 collective-permute-done.3.f4
  28.8 0.7 shard_map.130.r_1_
  29.5 6.9 %collective-permute-start.4 = (bf16[256,768]{1,0:T(8,128)(2,1)S(1)}, bf16[256,768]{1,0:T(8,128)(2,1)}, u32[]{:S(2)}, u32[]{:S(2)}) collective-permute-start(bf16[256,768]{1,0:T(8,128)(2,1)S(1)} %shard_map.130.r_1_), channel_id=1, source_target_pairs={{0,1},{1,0},{2,3},{3,2},{4,5},{5,4},{6,7},{7,6},{8,9},{9,8},{10,11... | collective-permute-start | bytes 1179656 | tf_op jit(solution)/shard_map/ppermute | solution.py:33
  36.4 0.0 collective-permute-done.12.r_5_
  36.4 0.0 collective-permute-start.5
  36.5 0.0 collective-permute-done.13.r_6_
  36.5 0.4 collective-permute-start.6
  36.9 0.0 collective-permute-done.14.r_7_
  36.9 3.1 %collective-permute-start.7 = (bf16[256,768]{1,0:T(8,128)(2,1)S(1)}, bf16[256,768]{1,0:T(8,128)(2,1)}, u32[]{:S(2)}, u32[]{:S(2)}) collective-permute-start(bf16[256,768]{1,0:T(8,128)(2,1)S(1)} %shard_map.130.r_1_), channel_id=1, source_target_pairs={{0,192},{64,128},{128,64},{192,0},{1,193},{65,129},{129,65},{193,1... | collective-permute-start | bytes 1179656 | tf_op jit(solution)/shard_map/ppermute | solution.py:33
  39.9 0.0 copy-done.2
  39.9 0.7 shard_map.134
  40.7 0.0 collective-permute-done.15.r_8_
  40.7 1.0 %shard_map.135 = (bf16[256,1536]{1,0:T(8,128)(2,1)S(1)}, f32[256,128]{1,0:T(8,128)S(1)}) custom-call(bf16[256,768]{1,0:T(8,128)(2,1)S(1)} %copy-done, bf16[256,768]{1,0:T(8,128)(2,1)S(1)} %get-tuple-element.26.own.r_7_.r_2_.r_1_, f32[256,768]{1,0:T(8,128)S(1)} %get-tuple-element.27.r_2_, f32[256,768]{1,0:T(8,128)S(1)} %get-tuple-element.28.r_3_, ...), custom_call_target="tpu_custom_call" | custom-call | flops 301989888 | bytes 6578176 | tf_op jit(solution)/shard_map/pallas_call | solution.py:49
  41.6 16.6 %all_to_all.15 = f32[32,8,128]{2,1,0:T(8,128)S(1)} all-to-all(f32[32,8,128]{2,1,0:T(8,128)S(1)} %bitcast.5), channel_id=1, replica_groups=mesh['r'=4,'x'=4,'z'=8,'c'=2] {'r','x','c'}, dimensions={0} | all-to-all | bytes 262144 | tf_op jit(solution)/shard_map/all_to_all | solution.py:330
  58.3 12.0 %all_to_all.16 = f32[8,8,128]{2,1,0:T(8,128)S(1)} all-to-all(f32[8,8,128]{2,1,0:T(8,128)S(1)} %broadcast_in_dim.6), channel_id=1, replica_groups=mesh['r'=4,'x'=4,'z'=8,'c'=2] {'z'}, dimensions={0} | all-to-all | bytes 65536 | tf_op jit(solution)/shard_map/all_to_all | solution.py:332
  70.3 0.7 broadcast_in_dim.7
  71.0 5.2 %all-to-all-start.2 = ((f32[32,8,128]{2,1,0:T(8,128)}), f32[32,8,128]{2,1,0:T(8,128)S(1)}, u32[]{:S(2)}, u32[]{:S(2)}) async-start(f32[32,8,128]{2,1,0:T(8,128)} %broadcast_in_dim.7), calls=%async_computation.2 | async-start | bytes 262144 | tf_op jit(solution)/shard_map/all_to_all | solution.py:334
  76.2 1.5 %shard_map.136 = bf16[256,768]{1,0:T(8,128)(2,1)} custom-call(bf16[256,768]{1,0:T(8,128)(2,1)S(1)} %copy-done.1, bf16[256,1536]{1,0:T(8,128)(2,1)S(1)} %get-tuple-element.42.r_1_, bf16[2,64,128]{2,1,0:T(8,128)(2,1)S(1)} %copy-done.4), custom_call_target="tpu_custom_call" | custom-call | flops 201326592 | bytes 1605632 | tf_op jit(solution)/shard_map/pallas_call | solution.py:49
  77.7 0.0 collective-permute-done.4.r_2_
  77.7 0.0 collective-permute-done.5.r_3_
  77.7 0.0 collective-permute-done.6.r_4_
  77.7 0.0 collective-permute-done.7.r_5_
  77.7 3.3 %shard_map.131 = bf16[256,768]{1,0:T(8,128)(2,1)} custom-call(bf16[5,256,256]{2,1,0:T(8,128)(2,1)S(1)} %shard_map.128.adj.r_0_, bf16[256,768]{1,0:T(8,128)(2,1)S(1)} %shard_map.130.r_1_, bf16[256,768]{1,0:T(8,128)(2,1)} %collective-permute-done.4.r_2_, bf16[256,768]{1,0:T(8,128)(2,1)} %collective-permute-done.5.r_3_, ...), custom_call_target="tpu_custom_call" | custom-call | flops 805306368 | bytes 3825664 | tf_op jit(solution)/shard_map/pallas_call | solution.py:49
  81.0 3.0 %all-to-all-done.2 = f32[32,8,128]{2,1,0:T(8,128)S(1)} async-done(((f32[32,8,128]{2,1,0:T(8,128)}), f32[32,8,128]{2,1,0:T(8,128)S(1)}, u32[]{:S(2)}, u32[]{:S(2)}) %all-to-all-start.2) | async-done | bytes 131104 | tf_op jit(solution)/shard_map/all_to_all | solution.py:334
  84.0 0.7 shard_map.137
  (3 shorter events, 0.1 us)
Async XLA Ops:
  0.6 0.7 copy-start.5
  0.6 0.7 copy-start.6
  1.3 1.0 %copy-start.3 = (bf16[12,128,128]{2,1,0:T(8,128)(2,1)S(1)}, bf16[12,128,128]{2,1,0:T(8,128)(2,1)}, u32[]{:S(2)}) copy-start(bf16[12,128,128]{2,1,0:T(8,128)(2,1)} %tiles.1) | copy-start | bytes 1179652
  2.3 1.0 %copy-start.1 = (bf16[256,768]{1,0:T(8,128)(2,1)S(1)}, bf16[256,768]{1,0:T(8,128)(2,1)}, u32[]{:S(2)}) copy-start(bf16[256,768]{1,0:T(8,128)(2,1)} %r_0_.7) | copy-start | bytes 1179652
  3.3 7.6 %copy-start = (bf16[256,768]{1,0:T(8,128)(2,1)S(1)}, bf16[256,768]{1,0:T(8,128)(2,1)}, u32[]{:S(2)}) copy-start(bf16[256,768]{1,0:T(8,128)(2,1)} %r_0_.6) | copy-start | bytes 1179652
  3.3 7.6 %copy-start.4 = (bf16[2,64,128]{2,1,0:T(8,128)(2,1)S(1)}, bf16[2,64,128]{2,1,0:T(8,128)(2,1)}, u32[]{:S(2)}) copy-start(bf16[2,64,128]{2,1,0:T(8,128)(2,1)} %r_2_.1) | copy-start | bytes 98308
  4.1 14.3 %collective-permute-start.10 = (bf16[256,768]{1,0:T(8,128)(2,1)S(1)}, bf16[256,768]{1,0:T(8,128)(2,1)S(1)}, u32[]{:S(2)}, u32[]{:S(2)}) collective-permute-start(bf16[256,768]{1,0:T(8,128)(2,1)S(1)} %get-tuple-element.32), channel_id=1, source_target_pairs={{0,64},{64,0},{128,192},{192,128},{1,65},{65,1},{129,193},{193,129... | collective-permute-start | bytes 1179656 | tf_op jit(solution)/shard_map/ppermute | solution.py:33
  6.3 12.1 %collective-permute-start.11 = (bf16[256,768]{1,0:T(8,128)(2,1)S(1)}, bf16[256,768]{1,0:T(8,128)(2,1)S(1)}, u32[]{:S(2)}, u32[]{:S(2)}) collective-permute-start(bf16[256,768]{1,0:T(8,128)(2,1)S(1)} %get-tuple-element.33), channel_id=1, source_target_pairs={{0,192},{64,128},{128,64},{192,0},{1,193},{65,129},{129,65},{193,1... | collective-permute-start | bytes 1179656 | tf_op jit(solution)/shard_map/ppermute | solution.py:33
  8.2 11.2 %collective-permute-start.8 = (bf16[256,768]{1,0:T(8,128)(2,1)S(1)}, bf16[256,768]{1,0:T(8,128)(2,1)S(1)}, u32[]{:S(2)}, u32[]{:S(2)}) collective-permute-start(bf16[256,768]{1,0:T(8,128)(2,1)S(1)} %get-tuple-element.30), channel_id=1, source_target_pairs={{0,1},{1,0},{2,3},{3,2},{4,5},{5,4},{6,7},{7,6},{8,9},{9,8},{10,11... | collective-permute-start | bytes 1179656 | tf_op jit(solution)/shard_map/ppermute | solution.py:33
  9.4 1.5 %copy-start.7 = (f32[128]{0:T(128)S(1)}, f32[128]{0:T(128)}, u32[]{:S(2)}) copy-start(f32[128]{0:T(128)} %param.12) | copy-start | bytes 1540
  9.4 11.8 %collective-permute-start.9 = (bf16[256,768]{1,0:T(8,128)(2,1)S(1)}, bf16[256,768]{1,0:T(8,128)(2,1)S(1)}, u32[]{:S(2)}, u32[]{:S(2)}) collective-permute-start(bf16[256,768]{1,0:T(8,128)(2,1)S(1)} %get-tuple-element.31), channel_id=1, source_target_pairs={{0,63},{1,2},{2,1},{3,4},{4,3},{5,6},{6,5},{7,8},{8,7},{9,10},{10,... | collective-permute-start | bytes 1179656 | tf_op jit(solution)/shard_map/ppermute | solution.py:33
  11.6 16.3 %collective-permute-start = (bf16[256,768]{1,0:T(8,128)(2,1)S(1)}, bf16[256,768]{1,0:T(8,128)(2,1)S(1)}, u32[]{:S(2)}, u32[]{:S(2)}) collective-permute-start(bf16[256,768]{1,0:T(8,128)(2,1)S(1)} %get-tuple-element.26.own.r_7_.r_2_.r_1_), channel_id=1, source_target_pairs={{0,1},{1,0},{2,3},{3,2},{4,5},{5,4},{6,7},{7,6},{8,9},{9,8},{10,11... | collective-permute-start | bytes 1179656 | tf_op jit(solution)/shard_map/ppermute | solution.py:33
  18.3 9.5 %collective-permute-start.1 = (bf16[256,768]{1,0:T(8,128)(2,1)S(1)}, bf16[256,768]{1,0:T(8,128)(2,1)S(1)}, u32[]{:S(2)}, u32[]{:S(2)}) collective-permute-start(bf16[256,768]{1,0:T(8,128)(2,1)S(1)} %get-tuple-element.26.own.r_7_.r_2_.r_1_), channel_id=1, source_target_pairs={{0,63},{1,2},{2,1},{3,4},{4,3},{5,6},{6,5},{7,8},{8,7},{9,10},{10,... | collective-permute-start | bytes 1179656 | tf_op jit(solution)/shard_map/ppermute | solution.py:33
  18.3 10.0 %collective-permute-start.2 = (bf16[256,768]{1,0:T(8,128)(2,1)S(1)}, bf16[256,768]{1,0:T(8,128)(2,1)S(1)}, u32[]{:S(2)}, u32[]{:S(2)}) collective-permute-start(bf16[256,768]{1,0:T(8,128)(2,1)S(1)} %get-tuple-element.26.own.r_7_.r_2_.r_1_), channel_id=1, source_target_pairs={{0,64},{64,0},{128,192},{192,128},{1,65},{65,1},{129,193},{193,129... | collective-permute-start | bytes 1179656 | tf_op jit(solution)/shard_map/ppermute | solution.py:33
  19.3 9.5 %collective-permute-start.3 = (bf16[256,768]{1,0:T(8,128)(2,1)S(1)}, bf16[256,768]{1,0:T(8,128)(2,1)S(1)}, u32[]{:S(2)}, u32[]{:S(2)}) collective-permute-start(bf16[256,768]{1,0:T(8,128)(2,1)S(1)} %get-tuple-element.26.own.r_7_.r_2_.r_1_), channel_id=1, source_target_pairs={{0,192},{64,128},{128,64},{192,0},{1,193},{65,129},{129,65},{193,1... | collective-permute-start | bytes 1179656 | tf_op jit(solution)/shard_map/ppermute | solution.py:33
  22.1 14.3 %collective-permute-start.12 = (bf16[256,768]{1,0:T(8,128)(2,1)S(1)}, bf16[256,768]{1,0:T(8,128)(2,1)S(1)}, u32[]{:S(2)}, u32[]{:S(2)}) collective-permute-start(bf16[256,768]{1,0:T(8,128)(2,1)S(1)} %get-tuple-element.35), channel_id=1, source_target_pairs={{0,1},{1,0},{2,3},{3,2},{4,5},{5,4},{6,7},{7,6},{8,9},{9,8},{10,11... | collective-permute-start | bytes 1179656 | tf_op jit(solution)/shard_map/ppermute | solution.py:33
  27.9 8.6 %collective-permute-start.13 = (bf16[256,768]{1,0:T(8,128)(2,1)S(1)}, bf16[256,768]{1,0:T(8,128)(2,1)S(1)}, u32[]{:S(2)}, u32[]{:S(2)}) collective-permute-start(bf16[256,768]{1,0:T(8,128)(2,1)S(1)} %get-tuple-element.36), channel_id=1, source_target_pairs={{0,63},{1,2},{2,1},{3,4},{4,3},{5,6},{6,5},{7,8},{8,7},{9,10},{10,... | collective-permute-start | bytes 1179656 | tf_op jit(solution)/shard_map/ppermute | solution.py:33
  27.9 9.0 %collective-permute-start.14 = (bf16[256,768]{1,0:T(8,128)(2,1)S(1)}, bf16[256,768]{1,0:T(8,128)(2,1)S(1)}, u32[]{:S(2)}, u32[]{:S(2)}) collective-permute-start(bf16[256,768]{1,0:T(8,128)(2,1)S(1)} %get-tuple-element.37), channel_id=1, source_target_pairs={{0,64},{64,0},{128,192},{192,128},{1,65},{65,1},{129,193},{193,129... | collective-permute-start | bytes 1179656 | tf_op jit(solution)/shard_map/ppermute | solution.py:33
  28.4 11.6 %copy-start.2 = (bf16[3,64,64]{2,1,0:T(8,128)(2,1)S(1)}, bf16[3,64,64]{2,1,0:T(8,128)(2,1)}, u32[]{:S(2)}) copy-start(bf16[3,64,64]{2,1,0:T(8,128)(2,1)} %r_11_.1) | copy-start | bytes 73732
  28.4 12.3 %collective-permute-start.15 = (bf16[256,768]{1,0:T(8,128)(2,1)S(1)}, bf16[256,768]{1,0:T(8,128)(2,1)S(1)}, u32[]{:S(2)}, u32[]{:S(2)}) collective-permute-start(bf16[256,768]{1,0:T(8,128)(2,1)S(1)} %get-tuple-element.38), channel_id=1, source_target_pairs={{0,192},{64,128},{128,64},{192,0},{1,193},{65,129},{129,65},{193,1... | collective-permute-start | bytes 1179656 | tf_op jit(solution)/shard_map/ppermute | solution.py:33
  29.5 48.1 %collective-permute-start.4 = (bf16[256,768]{1,0:T(8,128)(2,1)S(1)}, bf16[256,768]{1,0:T(8,128)(2,1)}, u32[]{:S(2)}, u32[]{:S(2)}) collective-permute-start(bf16[256,768]{1,0:T(8,128)(2,1)S(1)} %shard_map.130.r_1_), channel_id=1, source_target_pairs={{0,1},{1,0},{2,3},{3,2},{4,5},{5,4},{6,7},{7,6},{8,9},{9,8},{10,11... | collective-permute-start | bytes 1179656 | tf_op jit(solution)/shard_map/ppermute | solution.py:33
  36.4 41.2 %collective-permute-start.5 = (bf16[256,768]{1,0:T(8,128)(2,1)S(1)}, bf16[256,768]{1,0:T(8,128)(2,1)}, u32[]{:S(2)}, u32[]{:S(2)}) collective-permute-start(bf16[256,768]{1,0:T(8,128)(2,1)S(1)} %shard_map.130.r_1_), channel_id=1, source_target_pairs={{0,63},{1,2},{2,1},{3,4},{4,3},{5,6},{6,5},{7,8},{8,7},{9,10},{10,... | collective-permute-start | bytes 1179656 | tf_op jit(solution)/shard_map/ppermute | solution.py:33
  36.5 41.2 %collective-permute-start.6 = (bf16[256,768]{1,0:T(8,128)(2,1)S(1)}, bf16[256,768]{1,0:T(8,128)(2,1)}, u32[]{:S(2)}, u32[]{:S(2)}) collective-permute-start(bf16[256,768]{1,0:T(8,128)(2,1)S(1)} %shard_map.130.r_1_), channel_id=1, source_target_pairs={{0,64},{64,0},{128,192},{192,128},{1,65},{65,1},{129,193},{193,129... | collective-permute-start | bytes 1179656 | tf_op jit(solution)/shard_map/ppermute | solution.py:33
  36.9 40.8 %collective-permute-start.7 = (bf16[256,768]{1,0:T(8,128)(2,1)S(1)}, bf16[256,768]{1,0:T(8,128)(2,1)}, u32[]{:S(2)}, u32[]{:S(2)}) collective-permute-start(bf16[256,768]{1,0:T(8,128)(2,1)S(1)} %shard_map.130.r_1_), channel_id=1, source_target_pairs={{0,192},{64,128},{128,64},{192,0},{1,193},{65,129},{129,65},{193,1... | collective-permute-start | bytes 1179656 | tf_op jit(solution)/shard_map/ppermute | solution.py:33
  71.0 13.0 %all-to-all-start.2 = ((f32[32,8,128]{2,1,0:T(8,128)}), f32[32,8,128]{2,1,0:T(8,128)S(1)}, u32[]{:S(2)}, u32[]{:S(2)}) async-start(f32[32,8,128]{2,1,0:T(8,128)} %broadcast_in_dim.7), calls=%async_computation.2 | async-start | bytes 262144 | tf_op jit(solution)/shard_map/all_to_all | solution.py:334

commit v3 on v2

--- a/solution.py
+++ b/solution.py
@@ -15,9 +15,14 @@
 ROWS = 256
 DIFF_ROWS = 128
 BIAS_ROW = 224
+HOP1_ORDER = (3, 4, 1, 2)
+HOP2_ORDER = (3, 4, 1, 2)
+BACK2_ORDER = (3, 4, 1, 2)
+BACK1_ORDER = (1, 2, 3, 4)
 
 VMEM = pl.BlockSpec(memory_space=pltpu.VMEM)
 SMEM = pl.BlockSpec(memory_space=pltpu.SMEM)
+AFTER = pl.BlockSpec(memory_space=pl.ANY)
 
 
 DOM = ("x", "z", "c")
@@ -41,6 +46,10 @@
         swap(even, "r", 0),
         swap(odd, "r", 1),
     )
+
+
+def ordered(arrived, order):
+    return [arrived[k - 1] for k in order]
 
 
 def call(body, outs, args, specs, flops, scratch=()):
@@ -243,14 +252,14 @@
 
 def hop_body(adj, own, f1, f2, f3, f4, out):
     total = dot(adj[0], own[...])
-    for n, f in ((1, f1), (2, f2), (3, f3), (4, f4)):
+    for n, f in zip(HOP1_ORDER, (f1, f2, f3, f4)):
         total = total + dot(adj[n], f[...])
     out[...] = total.astype(BF16)
 
 
 def mix_body(steps, adj, hop1, f1, f2, f3, f4, x, gated, dw, out):
     total = dot(adj[0], hop1[...])
-    for n, f in ((1, f1), (2, f2), (3, f3), (4, f4)):
+    for n, f in zip(HOP2_ORDER, (f1, f2, f3, f4)):
         total = total + dot(adj[n], f[...])
     hop2 = total.astype(BF16)
     t0, t1, t2 = diff_table(dw[0]), diff_table(dw[1]), diff_table(dw[2])
@@ -305,7 +314,7 @@
     u1, *parts, own = call(
         second_body,
         [field] * 5 + [field32],
-        (adj, own, *arrived),
+        (adj, own, *ordered(arrived, BACK1_ORDER)),
         [VMEM] * 6,
         mac * 5 * 2 * BLK,
     )
@@ -320,7 +329,7 @@
     dpre, partial = call(
         lambda *r: late_body(steps, *r),
         [((cells, 2 * width), BF16), ((ROWS, PAIR), F32)],
-        (x, gated, dfilt, dgate, own, *arrived, back, sums, dw),
+        (x, gated, dfilt, dgate, own, *ordered(arrived, BACK2_ORDER), back, sums, dw),
         [VMEM] * 12,
         mac * 6 * PAIR,
     )
@@ -341,12 +350,12 @@
         mac * 4 * PAIR,
     )
     (hop1,) = call(
-        hop_body, [field], (adj, gated, *trade([gated] * 4)), [VMEM] * 6, mac * 5 * 2 * BLK
+        hop_body, [field], (adj, gated, *ordered(trade([gated] * 4), HOP1_ORDER)), [VMEM] * 6, mac * 5 * 2 * BLK
     )
     (mixed,) = call(
         lambda *r: mix_body(steps, *r),
         [field],
-        (adj, hop1, *trade([hop1] * 4), x, gated, dw),
+        (adj, hop1, *ordered(trade([hop1] * 4), HOP2_ORDER), x, gated, dw),
         [VMEM] * 9,
         mac * 8 * 2 * BLK,
     )

time: 85 us -> 82.6 us (0.972)
  blocking collectives: 28.6 us -> 25.1 us
  waiting for transfers between devices: 3 us -> 4.78 us
    all_to_all x1, blocking collectives: 12 us -> 9.72 us  [local(): piece = jnp.sum(lax.all_to_all(piece, 'z', 0, 0, tiled=True), axis=0)]
    ppermute x16, waiting for transfers between devices: 0.04 us -> 1.83 us  [swap(): return lax.ppermute(block, axis, route)]
    all_to_all x1, blocking collectives: 16.6 us -> 15.4 us  [local(): lax.all_to_all(partial.reshape(width_p, rows, PAIR), plane, 0, 0, tiled=T...]
  transfers between devices with their start and end apart: 17 -> 17, of which waited for: 1 -> 2; matrix products, arithmetic and copies ran while one was open for 1% -> 1% of each run, Pallas kernels for 10% -> 11%
where the time goes in v3:
time: 82.6 us; the launch traced here: 82.3 us
  starting transfers between devices  38.1 us (46%)
  blocking collectives  25.1 us (30%)
  Pallas kernels  11 us (13%)
  waiting for transfers between devices  4.78 us (6%)
  local copies, waits for them, and re-layouts  1.76 us (2%)
  between operations  1.46 us (2%)
    ppermute x16, starting transfers between devices, swap(): return lax.ppermute(block, axis, route)  32.9 us
    all_to_all x1, blocking collectives, local(): lax.all_to_all(partial.reshape(width_p, rows, PAIR), plane, 0, 0, tiled=T...  15.4 us
    pallas_call x10, Pallas kernels, call(): pl.pallas_call(body, out_shape=[jax.ShapeDtypeStruct(s, d) for s, d in ou...  11 us
    all_to_all x1, blocking collectives, local(): piece = jnp.sum(lax.all_to_all(piece, 'z', 0, 0, tiled=True), axis=0)  9.72 us
    all_to_all x1, starting transfers between devices, local(): full = lax.all_to_all(piece, plane, 0, 0, tiled=True).reshape(ROWS, PAIR)  5.23 us
    all_to_all x1, waiting for transfers between devices, local(): full = lax.all_to_all(piece, plane, 0, 0, tiled=True).reshape(ROWS, PAIR)  2.95 us
    ppermute x16, waiting for transfers between devices, swap(): return lax.ppermute(block, axis, route)  1.83 us
  transfers between devices with their start and end apart: 17, of which 2 were waited for; matrix products, arithmetic and copies ran while one was open for 1% of the time, Pallas kernels for 11%

profile of v3, /device:TPU:1, one launch (start us, length us, event | category | flops | bytes accessed | tf_op | source)
XLA Modules:
  0.0 82.3 jit_solution(1998675523792033181)
XLA Ops:
  0.6 0.0 copy-start.5
  0.6 0.0 copy-start.6
  1.3 0.0 copy-done.5
  1.3 0.0 copy-done.6
  1.3 0.0 copy-start.3
  1.3 1.0 %copy-done.3 = bf16[12,128,128]{2,1,0:T(8,128)(2,1)S(1)} copy-done((bf16[12,128,128]{2,1,0:T(8,128)(2,1)S(1)}, bf16[12,128,128]{2,1,0:T(8,128)(2,1)}, u32[]{:S(2)}) %copy-start.3) | copy-done | bytes 393240
  2.3 0.0 copy-start.1
  2.3 0.9 %shard_map.128.adj.r_0_ = bf16[5,256,256]{2,1,0:T(8,128)(2,1)S(1)} custom-call(s32[1,12]{1,0:T(1,128)S(1)} %copy-done.5, s32[1,12]{1,0:T(1,128)S(1)} %copy-done.6, s32[1]{0:T(128)S(6)} %copy.14.count, bf16[12,128,128]{2,1,0:T(8,128)(2,1)S(1)} %copy-done.3), custom_call_target="tpu_custom_call" | custom-call | bytes 1048676 | tf_op jit(solution)/shard_map/pallas_call | solution.py:58
  3.2 0.1 copy-done.1
  3.3 0.0 copy-start
  3.3 0.0 copy-start.4
  3.3 0.7 shard_map.132
  4.1 2.2 %collective-permute-start.10 = (bf16[256,768]{1,0:T(8,128)(2,1)S(1)}, bf16[256,768]{1,0:T(8,128)(2,1)S(1)}, u32[]{:S(2)}, u32[]{:S(2)}) collective-permute-start(bf16[256,768]{1,0:T(8,128)(2,1)S(1)} %get-tuple-element.32), channel_id=1, source_target_pairs={{0,64},{64,0},{128,192},{192,128},{1,65},{65,1},{129,193},{193,129... | collective-permute-start | bytes 1179656 | tf_op jit(solution)/shard_map/ppermute | solution.py:38
  6.3 1.9 %collective-permute-start.11 = (bf16[256,768]{1,0:T(8,128)(2,1)S(1)}, bf16[256,768]{1,0:T(8,128)(2,1)S(1)}, u32[]{:S(2)}, u32[]{:S(2)}) collective-permute-start(bf16[256,768]{1,0:T(8,128)(2,1)S(1)} %get-tuple-element.33), channel_id=1, source_target_pairs={{0,192},{64,128},{128,64},{192,0},{1,193},{65,129},{129,65},{193,1... | collective-permute-start | bytes 1179656 | tf_op jit(solution)/shard_map/ppermute | solution.py:38
  8.2 1.2 %collective-permute-start.8 = (bf16[256,768]{1,0:T(8,128)(2,1)S(1)}, bf16[256,768]{1,0:T(8,128)(2,1)S(1)}, u32[]{:S(2)}, u32[]{:S(2)}) collective-permute-start(bf16[256,768]{1,0:T(8,128)(2,1)S(1)} %get-tuple-element.30), channel_id=1, source_target_pairs={{0,1},{1,0},{2,3},{3,2},{4,5},{5,4},{6,7},{7,6},{8,9},{9,8},{10,11... | collective-permute-start | bytes 1179656 | tf_op jit(solution)/shard_map/ppermute | solution.py:38
  9.4 0.0 copy-start.7
  9.4 1.5 %collective-permute-start.9 = (bf16[256,768]{1,0:T(8,128)(2,1)S(1)}, bf16[256,768]{1,0:T(8,128)(2,1)S(1)}, u32[]{:S(2)}, u32[]{:S(2)}) collective-permute-start(bf16[256,768]{1,0:T(8,128)(2,1)S(1)} %get-tuple-element.31), channel_id=1, source_target_pairs={{0,63},{1,2},{2,1},{3,4},{4,3},{5,6},{6,5},{7,8},{8,7},{9,10},{10,... | collective-permute-start | bytes 1179656 | tf_op jit(solution)/shard_map/ppermute | solution.py:38
  10.9 0.0 copy-done
  10.9 0.0 copy-done.4
  10.9 0.0 copy-done.7
  10.9 0.6 shard_map.129
  11.6 0.5 collective-permute-start
  12.1 1.8 %collective-permute-done.10.p3 = bf16[256,768]{1,0:T(8,128)(2,1)S(1)} collective-permute-done((bf16[256,768]{1,0:T(8,128)(2,1)S(1)}, bf16[256,768]{1,0:T(8,128)(2,1)S(1)}, u32[]{:S(2)}, u32[]{:S(2)}) %collective-permute-start.10) | collective-permute-done | bytes 393248 | tf_op jit(solution)/shard_map/ppermute | solution.py:38
  13.9 3.8 %collective-permute-start.1 = (bf16[256,768]{1,0:T(8,128)(2,1)S(1)}, bf16[256,768]{1,0:T(8,128)(2,1)S(1)}, u32[]{:S(2)}, u32[]{:S(2)}) collective-permute-start(bf16[256,768]{1,0:T(8,128)(2,1)S(1)} %get-tuple-element.26.own.r_7_.r_2_.r_1_), channel_id=1, source_target_pairs={{0,192},{64,128},{128,64},{192,0},{1,193},{65,129},{129,65},{193,1... | collective-permute-start | bytes 1179656 | tf_op jit(solution)/shard_map/ppermute | solution.py:38
  17.7 0.0 collective-permute-done.11.p4
  17.7 3.0 %collective-permute-start.2 = (bf16[256,768]{1,0:T(8,128)(2,1)S(1)}, bf16[256,768]{1,0:T(8,128)(2,1)S(1)}, u32[]{:S(2)}, u32[]{:S(2)}) collective-permute-start(bf16[256,768]{1,0:T(8,128)(2,1)S(1)} %get-tuple-element.26.own.r_7_.r_2_.r_1_), channel_id=1, source_target_pairs={{0,1},{1,0},{2,3},{3,2},{4,5},{5,4},{6,7},{7,6},{8,9},{9,8},{10,11... | collective-permute-start | bytes 1179656 | tf_op jit(solution)/shard_map/ppermute | solution.py:38
  20.7 0.0 collective-permute-done.8.p1
  20.7 1.6 %collective-permute-start.3 = (bf16[256,768]{1,0:T(8,128)(2,1)S(1)}, bf16[256,768]{1,0:T(8,128)(2,1)S(1)}, u32[]{:S(2)}, u32[]{:S(2)}) collective-permute-start(bf16[256,768]{1,0:T(8,128)(2,1)S(1)} %get-tuple-element.26.own.r_7_.r_2_.r_1_), channel_id=1, source_target_pairs={{0,63},{1,2},{2,1},{3,4},{4,3},{5,6},{6,5},{7,8},{8,7},{9,10},{10,... | collective-permute-start | bytes 1179656 | tf_op jit(solution)/shard_map/ppermute | solution.py:38
  22.3 0.0 collective-permute-done.9.p2
  22.3 0.9 %shard_map.133 = (bf16[256,768]{1,0:T(8,128)(2,1)S(1)}, bf16[256,768]{1,0:T(8,128)(2,1)S(1)}, bf16[256,768]{1,0:T(8,128)(2,1)S(1)}, bf16[256,768]{1,0:T(8,128)(2...) custom-call(bf16[5,256,256]{2,1,0:T(8,128)(2,1)S(1)} %shard_map.128.adj.r_0_, ...), custom_call_target="tpu_custom_call" | custom-call | flops 503316480 | bytes 5767168 | tf_op jit(solution)/shard_map/pallas_call | solution.py:58
  23.2 0.1 collective-permute-start.12
  23.3 0.0 collective-permute-done.f1
  23.3 0.6 collective-permute-start.13
  23.9 0.0 collective-permute-done.1.f2
  23.9 7.1 %collective-permute-start.14 = (bf16[256,768]{1,0:T(8,128)(2,1)S(1)}, bf16[256,768]{1,0:T(8,128)(2,1)S(1)}, u32[]{:S(2)}, u32[]{:S(2)}) collective-permute-start(bf16[256,768]{1,0:T(8,128)(2,1)S(1)} %get-tuple-element.37), channel_id=1, source_target_pairs={{0,1},{1,0},{2,3},{3,2},{4,5},{5,4},{6,7},{7,6},{8,9},{9,8},{10,11... | collective-permute-start | bytes 1179656 | tf_op jit(solution)/shard_map/ppermute | solution.py:38
  31.0 0.0 collective-permute-done.2.f3
  31.0 0.0 copy-start.2
  31.0 0.0 collective-permute-start.15
  31.0 0.0 collective-permute-done.3.f4
  31.0 0.7 shard_map.130.r_1_
  31.7 0.7 collective-permute-start.4
  32.4 0.0 collective-permute-done.12.r_5_
  32.4 2.3 %collective-permute-start.5 = (bf16[256,768]{1,0:T(8,128)(2,1)S(1)}, bf16[256,768]{1,0:T(8,128)(2,1)}, u32[]{:S(2)}, u32[]{:S(2)}) collective-permute-start(bf16[256,768]{1,0:T(8,128)(2,1)S(1)} %shard_map.130.r_1_), channel_id=1, source_target_pairs={{0,192},{64,128},{128,64},{192,0},{1,193},{65,129},{129,65},{193,1... | collective-permute-start | bytes 1179656 | tf_op jit(solution)/shard_map/ppermute | solution.py:38
  34.7 0.0 collective-permute-done.13.r_6_
  34.7 6.3 %collective-permute-start.6 = (bf16[256,768]{1,0:T(8,128)(2,1)S(1)}, bf16[256,768]{1,0:T(8,128)(2,1)}, u32[]{:S(2)}, u32[]{:S(2)}) collective-permute-start(bf16[256,768]{1,0:T(8,128)(2,1)S(1)} %shard_map.130.r_1_), channel_id=1, source_target_pairs={{0,1},{1,0},{2,3},{3,2},{4,5},{5,4},{6,7},{7,6},{8,9},{9,8},{10,11... | collective-permute-start | bytes 1179656 | tf_op jit(solution)/shard_map/ppermute | solution.py:38
  41.0 0.0 collective-permute-done.14.r_7_
  41.0 0.0 collective-permute-start.7
  41.0 0.0 copy-done.2
  41.0 0.7 shard_map.134
  41.8 0.0 collective-permute-done.15.r_8_
  41.8 1.0 %shard_map.135 = (bf16[256,1536]{1,0:T(8,128)(2,1)S(1)}, f32[256,128]{1,0:T(8,128)S(1)}) custom-call(bf16[256,768]{1,0:T(8,128)(2,1)S(1)} %copy-done, bf16[256,768]{1,0:T(8,128)(2,1)S(1)} %get-tuple-element.26.own.r_7_.r_2_.r_1_, f32[256,768]{1,0:T(8,128)S(1)} %get-tuple-element.27.r_2_, f32[256,768]{1,0:T(8,128)S(1)} %get-tuple-element.28.r_3_, ...), custom_call_target="tpu_custom_call" | custom-call | flops 301989888 | bytes 6578176 | tf_op jit(solution)/shard_map/pallas_call | solution.py:58
  42.8 15.4 %all_to_all.15 = f32[32,8,128]{2,1,0:T(8,128)S(1)} all-to-all(f32[32,8,128]{2,1,0:T(8,128)S(1)} %bitcast.5), channel_id=1, replica_groups=mesh['r'=4,'x'=4,'z'=8,'c'=2] {'r','x','c'}, dimensions={0} | all-to-all | bytes 262144 | tf_op jit(solution)/shard_map/all_to_all | solution.py:339
  58.2 9.7 %all_to_all.16 = f32[8,8,128]{2,1,0:T(8,128)S(1)} all-to-all(f32[8,8,128]{2,1,0:T(8,128)S(1)} %broadcast_in_dim.6), channel_id=1, replica_groups=mesh['r'=4,'x'=4,'z'=8,'c'=2] {'z'}, dimensions={0} | all-to-all | bytes 65536 | tf_op jit(solution)/shard_map/all_to_all | solution.py:341
  67.9 0.7 broadcast_in_dim.7
  68.6 5.2 %all-to-all-start.2 = ((f32[32,8,128]{2,1,0:T(8,128)}), f32[32,8,128]{2,1,0:T(8,128)S(1)}, u32[]{:S(2)}, u32[]{:S(2)}) async-start(f32[32,8,128]{2,1,0:T(8,128)} %broadcast_in_dim.7), calls=%async_computation.2 | async-start | bytes 262144 | tf_op jit(solution)/shard_map/all_to_all | solution.py:343
  73.8 1.5 %shard_map.136 = bf16[256,768]{1,0:T(8,128)(2,1)} custom-call(bf16[256,768]{1,0:T(8,128)(2,1)S(1)} %copy-done.1, bf16[256,1536]{1,0:T(8,128)(2,1)S(1)} %get-tuple-element.42.r_1_, bf16[2,64,128]{2,1,0:T(8,128)(2,1)S(1)} %copy-done.4), custom_call_target="tpu_custom_call" | custom-call | flops 201326592 | bytes 1605632 | tf_op jit(solution)/shard_map/pallas_call | solution.py:58
  75.3 0.0 collective-permute-done.4.r_2_
  75.3 0.0 collective-permute-done.5.r_3_
  75.3 0.0 collective-permute-done.6.r_4_
  75.3 0.0 collective-permute-done.7.r_5_
  75.3 3.3 %shard_map.131 = bf16[256,768]{1,0:T(8,128)(2,1)} custom-call(bf16[5,256,256]{2,1,0:T(8,128)(2,1)S(1)} %shard_map.128.adj.r_0_, bf16[256,768]{1,0:T(8,128)(2,1)S(1)} %shard_map.130.r_1_, bf16[256,768]{1,0:T(8,128)(2,1)} %collective-permute-done.4.r_2_, bf16[256,768]{1,0:T(8,128)(2,1)} %collective-permute-done.5.r_3_, ...), custom_call_target="tpu_custom_call" | custom-call | flops 805306368 | bytes 3825664 | tf_op jit(solution)/shard_map/pallas_call | solution.py:58
  78.6 3.0 %all-to-all-done.2 = f32[32,8,128]{2,1,0:T(8,128)S(1)} async-done(((f32[32,8,128]{2,1,0:T(8,128)}), f32[32,8,128]{2,1,0:T(8,128)S(1)}, u32[]{:S(2)}, u32[]{:S(2)}) %all-to-all-start.2) | async-done | bytes 131104 | tf_op jit(solution)/shard_map/all_to_all | solution.py:343
  81.6 0.7 shard_map.137
  (3 shorter events, 0.1 us)
Async XLA Ops:
  0.6 0.7 copy-start.5
  0.6 0.7 copy-start.6
  1.3 1.0 %copy-start.3 = (bf16[12,128,128]{2,1,0:T(8,128)(2,1)S(1)}, bf16[12,128,128]{2,1,0:T(8,128)(2,1)}, u32[]{:S(2)}) copy-start(bf16[12,128,128]{2,1,0:T(8,128)(2,1)} %tiles.1) | copy-start | bytes 1179652
  2.3 1.0 %copy-start.1 = (bf16[256,768]{1,0:T(8,128)(2,1)S(1)}, bf16[256,768]{1,0:T(8,128)(2,1)}, u32[]{:S(2)}) copy-start(bf16[256,768]{1,0:T(8,128)(2,1)} %r_0_.7) | copy-start | bytes 1179652
  3.3 7.6 %copy-start = (bf16[256,768]{1,0:T(8,128)(2,1)S(1)}, bf16[256,768]{1,0:T(8,128)(2,1)}, u32[]{:S(2)}) copy-start(bf16[256,768]{1,0:T(8,128)(2,1)} %r_0_.6) | copy-start | bytes 1179652
  3.3 7.6 %copy-start.4 = (bf16[2,64,128]{2,1,0:T(8,128)(2,1)S(1)}, bf16[2,64,128]{2,1,0:T(8,128)(2,1)}, u32[]{:S(2)}) copy-start(bf16[2,64,128]{2,1,0:T(8,128)(2,1)} %r_2_.1) | copy-start | bytes 98308
  4.1 9.8 %collective-permute-start.10 = (bf16[256,768]{1,0:T(8,128)(2,1)S(1)}, bf16[256,768]{1,0:T(8,128)(2,1)S(1)}, u32[]{:S(2)}, u32[]{:S(2)}) collective-permute-start(bf16[256,768]{1,0:T(8,128)(2,1)S(1)} %get-tuple-element.32), channel_id=1, source_target_pairs={{0,64},{64,0},{128,192},{192,128},{1,65},{65,1},{129,193},{193,129... | collective-permute-start | bytes 1179656 | tf_op jit(solution)/shard_map/ppermute | solution.py:38
  6.3 11.4 %collective-permute-start.11 = (bf16[256,768]{1,0:T(8,128)(2,1)S(1)}, bf16[256,768]{1,0:T(8,128)(2,1)S(1)}, u32[]{:S(2)}, u32[]{:S(2)}) collective-permute-start(bf16[256,768]{1,0:T(8,128)(2,1)S(1)} %get-tuple-element.33), channel_id=1, source_target_pairs={{0,192},{64,128},{128,64},{192,0},{1,193},{65,129},{129,65},{193,1... | collective-permute-start | bytes 1179656 | tf_op jit(solution)/shard_map/ppermute | solution.py:38
  8.2 12.5 %collective-permute-start.8 = (bf16[256,768]{1,0:T(8,128)(2,1)S(1)}, bf16[256,768]{1,0:T(8,128)(2,1)S(1)}, u32[]{:S(2)}, u32[]{:S(2)}) collective-permute-start(bf16[256,768]{1,0:T(8,128)(2,1)S(1)} %get-tuple-element.30), channel_id=1, source_target_pairs={{0,1},{1,0},{2,3},{3,2},{4,5},{5,4},{6,7},{7,6},{8,9},{9,8},{10,11... | collective-permute-start | bytes 1179656 | tf_op jit(solution)/shard_map/ppermute | solution.py:38
  9.4 1.5 %copy-start.7 = (f32[128]{0:T(128)S(1)}, f32[128]{0:T(128)}, u32[]{:S(2)}) copy-start(f32[128]{0:T(128)} %param.12) | copy-start | bytes 1540
  9.4 12.9 %collective-permute-start.9 = (bf16[256,768]{1,0:T(8,128)(2,1)S(1)}, bf16[256,768]{1,0:T(8,128)(2,1)S(1)}, u32[]{:S(2)}, u32[]{:S(2)}) collective-permute-start(bf16[256,768]{1,0:T(8,128)(2,1)S(1)} %get-tuple-element.31), channel_id=1, source_target_pairs={{0,63},{1,2},{2,1},{3,4},{4,3},{5,6},{6,5},{7,8},{8,7},{9,10},{10,... | collective-permute-start | bytes 1179656 | tf_op jit(solution)/shard_map/ppermute | solution.py:38
  11.6 11.7 %collective-permute-start = (bf16[256,768]{1,0:T(8,128)(2,1)S(1)}, bf16[256,768]{1,0:T(8,128)(2,1)S(1)}, u32[]{:S(2)}, u32[]{:S(2)}) collective-permute-start(bf16[256,768]{1,0:T(8,128)(2,1)S(1)} %get-tuple-element.26.own.r_7_.r_2_.r_1_), channel_id=1, source_target_pairs={{0,64},{64,0},{128,192},{192,128},{1,65},{65,1},{129,193},{193,129... | collective-permute-start | bytes 1179656 | tf_op jit(solution)/shard_map/ppermute | solution.py:38
  13.9 10.0 %collective-permute-start.1 = (bf16[256,768]{1,0:T(8,128)(2,1)S(1)}, bf16[256,768]{1,0:T(8,128)(2,1)S(1)}, u32[]{:S(2)}, u32[]{:S(2)}) collective-permute-start(bf16[256,768]{1,0:T(8,128)(2,1)S(1)} %get-tuple-element.26.own.r_7_.r_2_.r_1_), channel_id=1, source_target_pairs={{0,192},{64,128},{128,64},{192,0},{1,193},{65,129},{129,65},{193,1... | collective-permute-start | bytes 1179656 | tf_op jit(solution)/shard_map/ppermute | solution.py:38
  17.7 13.3 %collective-permute-start.2 = (bf16[256,768]{1,0:T(8,128)(2,1)S(1)}, bf16[256,768]{1,0:T(8,128)(2,1)S(1)}, u32[]{:S(2)}, u32[]{:S(2)}) collective-permute-start(bf16[256,768]{1,0:T(8,128)(2,1)S(1)} %get-tuple-element.26.own.r_7_.r_2_.r_1_), channel_id=1, source_target_pairs={{0,1},{1,0},{2,3},{3,2},{4,5},{5,4},{6,7},{7,6},{8,9},{9,8},{10,11... | collective-permute-start | bytes 1179656 | tf_op jit(solution)/shard_map/ppermute | solution.py:38
  20.7 10.3 %collective-permute-start.3 = (bf16[256,768]{1,0:T(8,128)(2,1)S(1)}, bf16[256,768]{1,0:T(8,128)(2,1)S(1)}, u32[]{:S(2)}, u32[]{:S(2)}) collective-permute-start(bf16[256,768]{1,0:T(8,128)(2,1)S(1)} %get-tuple-element.26.own.r_7_.r_2_.r_1_), channel_id=1, source_target_pairs={{0,63},{1,2},{2,1},{3,4},{4,3},{5,6},{6,5},{7,8},{8,7},{9,10},{10,... | collective-permute-start | bytes 1179656 | tf_op jit(solution)/shard_map/ppermute | solution.py:38
  23.2 9.3 %collective-permute-start.12 = (bf16[256,768]{1,0:T(8,128)(2,1)S(1)}, bf16[256,768]{1,0:T(8,128)(2,1)S(1)}, u32[]{:S(2)}, u32[]{:S(2)}) collective-permute-start(bf16[256,768]{1,0:T(8,128)(2,1)S(1)} %get-tuple-element.35), channel_id=1, source_target_pairs={{0,64},{64,0},{128,192},{192,128},{1,65},{65,1},{129,193},{193,129... | collective-permute-start | bytes 1179656 | tf_op jit(solution)/shard_map/ppermute | solution.py:38
  23.3 11.4 %collective-permute-start.13 = (bf16[256,768]{1,0:T(8,128)(2,1)S(1)}, bf16[256,768]{1,0:T(8,128)(2,1)S(1)}, u32[]{:S(2)}, u32[]{:S(2)}) collective-permute-start(bf16[256,768]{1,0:T(8,128)(2,1)S(1)} %get-tuple-element.36), channel_id=1, source_target_pairs={{0,192},{64,128},{128,64},{192,0},{1,193},{65,129},{129,65},{193,1... | collective-permute-start | bytes 1179656 | tf_op jit(solution)/shard_map/ppermute | solution.py:38
  23.9 17.1 %collective-permute-start.14 = (bf16[256,768]{1,0:T(8,128)(2,1)S(1)}, bf16[256,768]{1,0:T(8,128)(2,1)S(1)}, u32[]{:S(2)}, u32[]{:S(2)}) collective-permute-start(bf16[256,768]{1,0:T(8,128)(2,1)S(1)} %get-tuple-element.37), channel_id=1, source_target_pairs={{0,1},{1,0},{2,3},{3,2},{4,5},{5,4},{6,7},{7,6},{8,9},{9,8},{10,11... | collective-permute-start | bytes 1179656 | tf_op jit(solution)/shard_map/ppermute | solution.py:38
  31.0 10.0 %copy-start.2 = (bf16[3,64,64]{2,1,0:T(8,128)(2,1)S(1)}, bf16[3,64,64]{2,1,0:T(8,128)(2,1)}, u32[]{:S(2)}) copy-start(bf16[3,64,64]{2,1,0:T(8,128)(2,1)} %r_11_.1) | copy-start | bytes 73732
  31.0 10.8 %collective-permute-start.15 = (bf16[256,768]{1,0:T(8,128)(2,1)S(1)}, bf16[256,768]{1,0:T(8,128)(2,1)S(1)}, u32[]{:S(2)}, u32[]{:S(2)}) collective-permute-start(bf16[256,768]{1,0:T(8,128)(2,1)S(1)} %get-tuple-element.38), channel_id=1, source_target_pairs={{0,63},{1,2},{2,1},{3,4},{4,3},{5,6},{6,5},{7,8},{8,7},{9,10},{10,... | collective-permute-start | bytes 1179656 | tf_op jit(solution)/shard_map/ppermute | solution.py:38
  31.7 43.6 %collective-permute-start.4 = (bf16[256,768]{1,0:T(8,128)(2,1)S(1)}, bf16[256,768]{1,0:T(8,128)(2,1)}, u32[]{:S(2)}, u32[]{:S(2)}) collective-permute-start(bf16[256,768]{1,0:T(8,128)(2,1)S(1)} %shard_map.130.r_1_), channel_id=1, source_target_pairs={{0,64},{64,0},{128,192},{192,128},{1,65},{65,1},{129,193},{193,129... | collective-permute-start | bytes 1179656 | tf_op jit(solution)/shard_map/ppermute | solution.py:38
  32.4 42.8 %collective-permute-start.5 = (bf16[256,768]{1,0:T(8,128)(2,1)S(1)}, bf16[256,768]{1,0:T(8,128)(2,1)}, u32[]{:S(2)}, u32[]{:S(2)}) collective-permute-start(bf16[256,768]{1,0:T(8,128)(2,1)S(1)} %shard_map.130.r_1_), channel_id=1, source_target_pairs={{0,192},{64,128},{128,64},{192,0},{1,193},{65,129},{129,65},{193,1... | collective-permute-start | bytes 1179656 | tf_op jit(solution)/shard_map/ppermute | solution.py:38
  34.7 40.6 %collective-permute-start.6 = (bf16[256,768]{1,0:T(8,128)(2,1)S(1)}, bf16[256,768]{1,0:T(8,128)(2,1)}, u32[]{:S(2)}, u32[]{:S(2)}) collective-permute-start(bf16[256,768]{1,0:T(8,128)(2,1)S(1)} %shard_map.130.r_1_), channel_id=1, source_target_pairs={{0,1},{1,0},{2,3},{3,2},{4,5},{5,4},{6,7},{7,6},{8,9},{9,8},{10,11... | collective-permute-start | bytes 1179656 | tf_op jit(solution)/shard_map/ppermute | solution.py:38
  41.0 34.3 %collective-permute-start.7 = (bf16[256,768]{1,0:T(8,128)(2,1)S(1)}, bf16[256,768]{1,0:T(8,128)(2,1)}, u32[]{:S(2)}, u32[]{:S(2)}) collective-permute-start(bf16[256,768]{1,0:T(8,128)(2,1)S(1)} %shard_map.130.r_1_), channel_id=1, source_target_pairs={{0,63},{1,2},{2,1},{3,4},{4,3},{5,6},{6,5},{7,8},{8,7},{9,10},{10,... | collective-permute-start | bytes 1179656 | tf_op jit(solution)/shard_map/ppermute | solution.py:38
  68.6 13.0 %all-to-all-start.2 = ((f32[32,8,128]{2,1,0:T(8,128)}), f32[32,8,128]{2,1,0:T(8,128)S(1)}, u32[]{:S(2)}, u32[]{:S(2)}) async-start(f32[32,8,128]{2,1,0:T(8,128)} %broadcast_in_dim.7), calls=%async_computation.2 | async-start | bytes 262144 | tf_op jit(solution)/shard_map/all_to_all | solution.py:343

commit v4 on v3

--- a/solution.py
+++ b/solution.py
@@ -135,7 +135,9 @@
         adj[n, :, BLK:] = total[2 * n + 1].astype(BF16)
 
 
-def gate_body(steps, x, cw, cb, gated, dfilt, dgate):
+def gate_body(steps, x, cw, cb, g, dw, gated, dfilt, dgate, back, sums):
+    t0 = diff_table(dw[0])
+    acc = jnp.zeros((PAIR, PAIR), F32)
     table = conv_table(cw[0], cw[1])
     bias = cb[...]
     turned = half_turn(bias)
@@ -151,9 +153,13 @@
         opened = jax.nn.sigmoid(pre[:, PAIR:] + bias_g)
         cols = slice(j * PAIR, (j + 1) * PAIR)
         both = filt * opened
-        gated[:, cols] = both.astype(BF16)
+        hj = both.astype(BF16)
+        gated[:, cols] = hj
+        back[:, cols] = dot_nt(g[:, cols], t0)
+        acc = acc + dot_tn(hj, g[:, cols])
         dfilt[:, cols] = opened * (1.0 - filt * filt)
         dgate[:, cols] = both * (1.0 - opened)
+    sums[...] = acc
 
 
 def first_body(adj, g, *outs):
@@ -172,29 +178,17 @@
         out[...] = dot_tn(adj[n], field).astype(out.dtype)
 
 
-def early_body(steps, g, u1, gated, dw, back, sums):
-    t0 = diff_table(dw[0])
-    t1 = diff_table(dw[1])
-    acc = [jnp.zeros((PAIR, PAIR), F32) for _ in range(2)]
-    for j in range(steps // 2):
-        gj, uj, hj = pairs(g, j), pairs(u1, j), pairs(gated, j)
-        back[:, j * PAIR : (j + 1) * PAIR] = dot_nt(gj, t0) + dot_nt(uj, t1)
-        acc[0] = acc[0] + dot_tn(hj, gj)
-        acc[1] = acc[1] + dot_tn(hj, uj)
-    sums[0] = acc[0]
-    sums[1] = acc[1]
-
-
 def fold(q):
     return q[:CH] + half_turn(q[CH:])
 
 
 def late_body(
-    steps, x, gated, dfilt, dgate, own, p1, p2, p3, p4, back, sums, dw, dpre, partial
+    steps, x, gated, dfilt, dgate, own, p1, p2, p3, p4, back, sums, dw, u1, dpre, partial
 ):
-    t2 = diff_table(dw[2])
+    t1, t2 = diff_table(dw[1]), diff_table(dw[2])
     half = steps // 2
     acc = jnp.zeros((PAIR, PAIR), F32)
+    acc1 = jnp.zeros((PAIR, PAIR), F32)
     bias_f = jnp.zeros((1, PAIR), F32)
     bias_g = jnp.zeros((1, PAIR), F32)
     for j in range(half):
@@ -203,7 +197,8 @@
         for p in (p1, p2, p3, p4):
             u2 = u2 + p[:, cols].astype(F32)
         u2 = u2.astype(BF16)
-        back_zero = back[:, cols] + dot_nt(u2, t2)
+        back_zero = back[:, cols] + dot_nt(pairs(u1, j), t1) + dot_nt(u2, t2)
+        acc1 = acc1 + dot_tn(pairs(gated, j), pairs(u1, j))
         df = (back_zero * dfilt[:, cols]).astype(BF16)
         dg = (back_zero * dgate[:, cols]).astype(BF16)
         dpre[:, 2 * j * PAIR : (2 * j + 1) * PAIR] = df
@@ -227,7 +222,7 @@
     next_f, next_g = ahead[CH:, :PAIR], ahead[CH:, PAIR:]
     partial[:CH] = jnp.where(low, top_f + half_turn(bottom_f), half_turn(top_g) + bottom_g)
     partial[CH:PAIR] = jnp.where(low, half_turn(top_f) + next_f, top_g + half_turn(next_g))
-    q0, q1, q2 = fold(sums[0]), fold(sums[1]), fold(acc)
+    q0, q1, q2 = fold(sums[...]), fold(acc1), fold(acc)
     partial[DIFF_ROWS : DIFF_ROWS + CH] = jnp.where(low, q0, half_turn(q1))
     partial[DIFF_ROWS + CH : BIAS_ROW] = jnp.where(low[:32], q2[:32], half_turn(q2[32:]))
     bias = jnp.where(
@@ -270,6 +265,10 @@
         out[:, cols] = mixed.astype(BF16)
 
 
+def copies_body(parts, out):
+    out[...] = jnp.broadcast_to(jnp.sum(parts[...], axis=0, keepdims=True), out.shape)
+
+
 def finish_body(scale, full, diff, conv, bias):
     conv[0] = full[:CH] * scale
     conv[1] = full[CH:PAIR] * scale
@@ -304,11 +303,11 @@
         first_body, [field] * 4 + [field32], (adj, g), [VMEM] * 2, mac * 5 * 2 * BLK
     )
     arrived = trade(parts)
-    gated, dfilt, dgate = call(
+    gated, dfilt, dgate, back, sums = call(
         lambda *r: gate_body(steps, *r),
-        [field, field32, field32],
-        (x, cw, cb.reshape(1, -1)),
-        [VMEM] * 3,
+        [field, field32, field32, field32, ((PAIR, PAIR), F32)],
+        (x, cw, cb.reshape(1, -1), g, dw),
+        [VMEM] * 5,
         mac * 2 * PAIR,
     )
     u1, *parts, own = call(
@@ -319,18 +318,11 @@
         mac * 5 * 2 * BLK,
     )
     arrived = trade(parts)
-    back, sums = call(
-        lambda *r: early_body(steps, *r),
-        [field32, ((2, PAIR, PAIR), F32)],
-        (g, u1, gated, dw),
-        [VMEM] * 4,
-        mac * 4 * PAIR,
-    )
     dpre, partial = call(
         lambda *r: late_body(steps, *r),
         [((cells, 2 * width), BF16), ((ROWS, PAIR), F32)],
-        (x, gated, dfilt, dgate, own, *ordered(arrived, BACK2_ORDER), back, sums, dw),
-        [VMEM] * 12,
+        (x, gated, dfilt, dgate, own, *ordered(arrived, BACK2_ORDER), back, sums, dw, u1),
+        [VMEM] * 13,
         mac * 6 * PAIR,
     )
     plane, depth = ("r", "x", "c"), lax.axis_size("z")
@@ -338,8 +330,8 @@
     rows = ROWS // width_p
     piece = lax.all_to_all(partial.reshape(width_p, rows, PAIR), plane, 0, 0, tiled=True)
     piece = jnp.broadcast_to(jnp.sum(piece, axis=0), (depth, rows, PAIR))
-    piece = jnp.sum(lax.all_to_all(piece, "z", 0, 0, tiled=True), axis=0)
-    piece = jnp.broadcast_to(piece, (width_p, rows, PAIR))
+    piece = lax.all_to_all(piece, "z", 0, 0, tiled=True)
+    (piece,) = call(copies_body, [((width_p, rows, PAIR), F32)], (piece,), [VMEM], 0)
     full = lax.all_to_all(piece, plane, 0, 0, tiled=True).reshape(ROWS, PAIR)
 
     (grad_features,) = call(

time: 82.6 us -> 85.4 us (1.034)
  waiting for transfers between devices: 4.78 us -> 6.1 us
  blocking collectives: 25.1 us -> 26 us
    all_to_all x1, blocking collectives: 9.72 us -> 12.2 us  [local(): piece = lax.all_to_all(piece, 'z', 0, 0, tiled=True)]
    all_to_all x1, blocking collectives: 15.4 us -> 13.8 us  [local(): lax.all_to_all(partial.reshape(width_p, rows, PAIR), plane, 0, 0, tiled=T...]
    ppermute x16, waiting for transfers between devices: 1.83 us -> 3.26 us  [swap(): return lax.ppermute(block, axis, route)]
  transfers between devices with their start and end apart: 17 -> 17, of which waited for: 2 -> 3; matrix products, arithmetic and copies ran while one was open for 1% -> 0% of each run, Pallas kernels for 11% -> 11%
where the time goes in v4:
time: 85.4 us; the launch traced here: 85 us
  starting transfers between devices  38.8 us (45%)
  blocking collectives  26 us (30%)
  Pallas kernels  11.5 us (13%)
  waiting for transfers between devices  6.1 us (7%)
  between operations  1.43 us (2%)
  local copies, waits for them, and re-layouts  1.21 us (1%)
    ppermute x16, starting transfers between devices, swap(): return lax.ppermute(block, axis, route)  32.7 us
    all_to_all x1, blocking collectives, local(): lax.all_to_all(partial.reshape(width_p, rows, PAIR), plane, 0, 0, tiled=T...  13.8 us
    all_to_all x1, blocking collectives, local(): piece = lax.all_to_all(piece, 'z', 0, 0, tiled=True)  12.2 us
    pallas_call x10, Pallas kernels, call(): pl.pallas_call(body, out_shape=[jax.ShapeDtypeStruct(s, d) for s, d in ou...  11.5 us
    all_to_all x1, starting transfers between devices, local(): full = lax.all_to_all(piece, plane, 0, 0, tiled=True).reshape(ROWS, PAIR)  6.05 us
    ppermute x16, waiting for transfers between devices, swap(): return lax.ppermute(block, axis, route)  3.26 us
    all_to_all x1, waiting for transfers between devices, local(): full = lax.all_to_all(piece, plane, 0, 0, tiled=True).reshape(ROWS, PAIR)  2.84 us
  transfers between devices with their start and end apart: 17, of which 3 were waited for; matrix products, arithmetic and copies ran while one was open for 0% of the time, Pallas kernels for 11%

profile of v4, /device:TPU:1, one launch (start us, length us, event | category | flops | bytes accessed | tf_op | source)
XLA Modules:
  0.0 85.0 jit_solution(13875796581340515646)
XLA Ops:
  0.6 0.0 copy-start.6
  0.6 0.0 copy-start.5
  1.3 0.0 copy-done.6
  1.3 0.0 copy-done.5
  1.3 0.0 copy-start.3
  1.3 1.0 %copy-done.3 = bf16[12,128,128]{2,1,0:T(8,128)(2,1)S(1)} copy-done((bf16[12,128,128]{2,1,0:T(8,128)(2,1)S(1)}, bf16[12,128,128]{2,1,0:T(8,128)(2,1)}, u32[]{:S(2)}) %copy-start.3) | copy-done | bytes 393240
  2.3 0.0 copy-start.1
  2.3 0.8 shard_map.128.adj.r_0_
  3.1 0.2 copy-done.1
  3.3 0.0 copy-start
  3.3 0.0 copy-start.2
  3.3 0.0 copy-start.4
  3.3 0.7 shard_map.132
  4.1 3.3 %collective-permute-start.8 = (bf16[256,768]{1,0:T(8,128)(2,1)S(1)}, bf16[256,768]{1,0:T(8,128)(2,1)S(1)}, u32[]{:S(2)}, u32[]{:S(2)}) collective-permute-start(bf16[256,768]{1,0:T(8,128)(2,1)S(1)} %get-tuple-element.30), channel_id=1, source_target_pairs={{0,1},{1,0},{2,3},{3,2},{4,5},{5,4},{6,7},{7,6},{8,9},{9,8},{10,11... | collective-permute-start | bytes 1179656 | tf_op jit(solution)/shard_map/ppermute | solution.py:38
  7.4 0.0 collective-permute-start.9
  7.4 1.2 %collective-permute-start.10 = (bf16[256,768]{1,0:T(8,128)(2,1)S(1)}, bf16[256,768]{1,0:T(8,128)(2,1)S(1)}, u32[]{:S(2)}, u32[]{:S(2)}) collective-permute-start(bf16[256,768]{1,0:T(8,128)(2,1)S(1)} %get-tuple-element.32), channel_id=1, source_target_pairs={{0,64},{64,0},{128,192},{192,128},{1,65},{65,1},{129,193},{193,129... | collective-permute-start | bytes 1179656 | tf_op jit(solution)/shard_map/ppermute | solution.py:38
  8.6 0.0 copy-start.7
  8.6 1.9 %collective-permute-start.11 = (bf16[256,768]{1,0:T(8,128)(2,1)S(1)}, bf16[256,768]{1,0:T(8,128)(2,1)S(1)}, u32[]{:S(2)}, u32[]{:S(2)}) collective-permute-start(bf16[256,768]{1,0:T(8,128)(2,1)S(1)} %get-tuple-element.33), channel_id=1, source_target_pairs={{0,192},{64,128},{128,64},{192,0},{1,193},{65,129},{129,65},{193,1... | collective-permute-start | bytes 1179656 | tf_op jit(solution)/shard_map/ppermute | solution.py:38
  10.5 0.0 copy-done
  10.5 0.0 copy-done.2
  10.5 0.0 copy-done.4
  10.5 0.0 copy-done.7
  10.5 1.1 %shard_map.129 = (bf16[256,768]{1,0:T(8,128)(2,1)S(1)}, f32[256,768]{1,0:T(8,128)S(1)}, f32[256,768]{1,0:T(8,128)S(1)}, f32[256,768]{1,0:T(8,128)S(1)}, f32[128,128]{1,0:T(8,128)S(1)}) custom-call(bf16[256,768]{1,0:T(8,128)(2,1)S(1)} %copy-done, bf16[2,64,128]{2,1,0:T(8,128)(2,1)S(1)} %copy-done.4, f32[1,128]{1,0:T(1,128)S(1)} %bitcast.6, ...), custom_call_target="tpu_custom_call" | custom-call | flops 100663296 | bytes 3662336 | tf_op jit(solution)/shard_map/pallas_call | solution.py:58
  11.6 0.8 collective-permute-start.3
  12.4 0.0 collective-permute-done.8.p1
  12.4 6.5 %collective-permute-start.2 = (bf16[256,768]{1,0:T(8,128)(2,1)S(1)}, bf16[256,768]{1,0:T(8,128)(2,1)S(1)}, u32[]{:S(2)}, u32[]{:S(2)}) collective-permute-start(bf16[256,768]{1,0:T(8,128)(2,1)S(1)} %get-tuple-element.26.own.r_7_.r_1_), channel_id=1, source_target_pairs={{0,1},{1,0},{2,3},{3,2},{4,5},{5,4},{6,7},{7,6},{8,9},{9,8},{10,11... | collective-permute-start | bytes 1179656 | tf_op jit(solution)/shard_map/ppermute | solution.py:38
  18.9 0.0 collective-permute-done.9.p2
  18.9 0.8 collective-permute-start.1
  19.7 0.0 collective-permute-done.10.p3
  19.7 0.0 collective-permute-start
  19.7 0.0 collective-permute-done.11.p4
  19.7 0.9 %shard_map.133 = (bf16[256,768]{1,0:T(8,128)(2,1)S(1)}, bf16[256,768]{1,0:T(8,128)(2,1)S(1)}, bf16[256,768]{1,0:T(8,128)(2,1)S(1)}, bf16[256,768]{1,0:T(8,128)(2...) custom-call(bf16[5,256,256]{2,1,0:T(8,128)(2,1)S(1)} %shard_map.128.adj.r_0_, ...), custom_call_target="tpu_custom_call" | custom-call | flops 503316480 | bytes 5767168 | tf_op jit(solution)/shard_map/pallas_call | solution.py:58
  20.6 1.6 %collective-permute-start.12 = (bf16[256,768]{1,0:T(8,128)(2,1)S(1)}, bf16[256,768]{1,0:T(8,128)(2,1)S(1)}, u32[]{:S(2)}, u32[]{:S(2)}) collective-permute-start(bf16[256,768]{1,0:T(8,128)(2,1)S(1)} %get-tuple-element.35), channel_id=1, source_target_pairs={{0,64},{64,0},{128,192},{192,128},{1,65},{65,1},{129,193},{193,129... | collective-permute-start | bytes 1179656 | tf_op jit(solution)/shard_map/ppermute | solution.py:38
  22.1 0.0 collective-permute-done.3.f4
  22.1 1.9 %collective-permute-start.13 = (bf16[256,768]{1,0:T(8,128)(2,1)S(1)}, bf16[256,768]{1,0:T(8,128)(2,1)S(1)}, u32[]{:S(2)}, u32[]{:S(2)}) collective-permute-start(bf16[256,768]{1,0:T(8,128)(2,1)S(1)} %get-tuple-element.36), channel_id=1, source_target_pairs={{0,192},{64,128},{128,64},{192,0},{1,193},{65,129},{129,65},{193,1... | collective-permute-start | bytes 1179656 | tf_op jit(solution)/shard_map/ppermute | solution.py:38
  24.0 0.0 collective-permute-done.2.f3
  24.0 6.3 %collective-permute-start.14 = (bf16[256,768]{1,0:T(8,128)(2,1)S(1)}, bf16[256,768]{1,0:T(8,128)(2,1)S(1)}, u32[]{:S(2)}, u32[]{:S(2)}) collective-permute-start(bf16[256,768]{1,0:T(8,128)(2,1)S(1)} %get-tuple-element.37), channel_id=1, source_target_pairs={{0,1},{1,0},{2,3},{3,2},{4,5},{5,4},{6,7},{7,6},{8,9},{9,8},{10,11... | collective-permute-start | bytes 1179656 | tf_op jit(solution)/shard_map/ppermute | solution.py:38
  30.4 0.9 %collective-permute-done.1.f2 = bf16[256,768]{1,0:T(8,128)(2,1)S(1)} collective-permute-done((bf16[256,768]{1,0:T(8,128)(2,1)S(1)}, bf16[256,768]{1,0:T(8,128)(2,1)S(1)}, u32[]{:S(2)}, u32[]{:S(2)}) %collective-permute-start.1) | collective-permute-done | bytes 393248 | tf_op jit(solution)/shard_map/ppermute | solution.py:38
  31.3 0.0 collective-permute-start.15
  31.3 0.0 collective-permute-done.f1
  31.3 0.7 shard_map.130.r_1_
  32.0 1.8 %collective-permute-start.7 = (bf16[256,768]{1,0:T(8,128)(2,1)S(1)}, bf16[256,768]{1,0:T(8,128)(2,1)}, u32[]{:S(2)}, u32[]{:S(2)}) collective-permute-start(bf16[256,768]{1,0:T(8,128)(2,1)S(1)} %shard_map.130.r_1_), channel_id=1, source_target_pairs={{0,63},{1,2},{2,1},{3,4},{4,3},{5,6},{6,5},{7,8},{8,7},{9,10},{10,... | collective-permute-start | bytes 1179656 | tf_op jit(solution)/shard_map/ppermute | solution.py:38
  33.9 2.3 %collective-permute-done.12.r_5_ = bf16[256,768]{1,0:T(8,128)(2,1)S(1)} collective-permute-done((bf16[256,768]{1,0:T(8,128)(2,1)S(1)}, bf16[256,768]{1,0:T(8,128)(2,1)S(1)}, u32[]{:S(2)}, u32[]{:S(2)}) %collective-permute-start.12) | collective-permute-done | bytes 393248 | tf_op jit(solution)/shard_map/ppermute | solution.py:38
  36.1 3.6 %collective-permute-start.6 = (bf16[256,768]{1,0:T(8,128)(2,1)S(1)}, bf16[256,768]{1,0:T(8,128)(2,1)}, u32[]{:S(2)}, u32[]{:S(2)}) collective-permute-start(bf16[256,768]{1,0:T(8,128)(2,1)S(1)} %shard_map.130.r_1_), channel_id=1, source_target_pairs={{0,1},{1,0},{2,3},{3,2},{4,5},{5,4},{6,7},{7,6},{8,9},{9,8},{10,11... | collective-permute-start | bytes 1179656 | tf_op jit(solution)/shard_map/ppermute | solution.py:38
  39.7 0.0 collective-permute-done.13.r_6_
  39.7 3.0 %collective-permute-start.5 = (bf16[256,768]{1,0:T(8,128)(2,1)S(1)}, bf16[256,768]{1,0:T(8,128)(2,1)}, u32[]{:S(2)}, u32[]{:S(2)}) collective-permute-start(bf16[256,768]{1,0:T(8,128)(2,1)S(1)} %shard_map.130.r_1_), channel_id=1, source_target_pairs={{0,192},{64,128},{128,64},{192,0},{1,193},{65,129},{129,65},{193,1... | collective-permute-start | bytes 1179656 | tf_op jit(solution)/shard_map/ppermute | solution.py:38
  42.8 0.0 collective-permute-done.14.r_7_
  42.8 0.0 collective-permute-start.4
  42.8 0.0 collective-permute-done.15.r_8_
  42.8 1.1 %shard_map.134 = (bf16[256,1536]{1,0:T(8,128)(2,1)S(1)}, f32[256,128]{1,0:T(8,128)S(1)}) custom-call(bf16[256,768]{1,0:T(8,128)(2,1)S(1)} %copy-done, bf16[256,768]{1,0:T(8,128)(2,1)S(1)} %get-tuple-element.26.own.r_7_.r_1_, f32[256,768]{1,0:T(8,128)S(1)} %get-tuple-element.27.r_2_, f32[256,768]{1,0:T(8,128)S(1)} %get-tuple-element.28.r_3_, ...), custom_call_target="tpu_custom_call" | custom-call | flops 301989888 | bytes 6905856 | tf_op jit(solution)/shard_map/pallas_call | solution.py:58
  43.9 13.8 %all_to_all.15 = f32[32,8,128]{2,1,0:T(8,128)S(1)} all-to-all(f32[32,8,128]{2,1,0:T(8,128)S(1)} %bitcast.5), channel_id=1, replica_groups=mesh['r'=4,'x'=4,'z'=8,'c'=2] {'r','x','c'}, dimensions={0} | all-to-all | bytes 262144 | tf_op jit(solution)/shard_map/all_to_all | solution.py:331
  57.7 12.2 %all_to_all.16.parts = f32[8,8,128]{2,1,0:T(8,128)S(1)} all-to-all(f32[8,8,128]{2,1,0:T(8,128)S(1)} %broadcast_in_dim.3), channel_id=1, replica_groups=mesh['r'=4,'x'=4,'z'=8,'c'=2] {'z'}, dimensions={0} | all-to-all | bytes 65536 | tf_op jit(solution)/shard_map/all_to_all | solution.py:333
  70.0 0.7 shard_map.136
  70.6 6.0 %all-to-all-start.2 = ((f32[32,8,128]{2,1,0:T(8,128)}), f32[32,8,128]{2,1,0:T(8,128)S(1)}, u32[]{:S(2)}, u32[]{:S(2)}) async-start(f32[32,8,128]{2,1,0:T(8,128)} %shard_map.136), calls=%async_computation.2 | async-start | bytes 262144 | tf_op jit(solution)/shard_map/all_to_all | solution.py:335
  76.7 1.5 %shard_map.135 = bf16[256,768]{1,0:T(8,128)(2,1)} custom-call(bf16[256,768]{1,0:T(8,128)(2,1)S(1)} %copy-done.1, bf16[256,1536]{1,0:T(8,128)(2,1)S(1)} %get-tuple-element.42.r_1_, bf16[2,64,128]{2,1,0:T(8,128)(2,1)S(1)} %copy-done.4), custom_call_target="tpu_custom_call" | custom-call | flops 201326592 | bytes 1605632 | tf_op jit(solution)/shard_map/pallas_call | solution.py:58
  78.1 0.0 collective-permute-done.7.r_5_
  78.1 0.0 collective-permute-done.6.r_4_
  78.1 0.0 collective-permute-done.5.r_3_
  78.1 0.0 collective-permute-done.4.r_2_
  78.2 3.3 %shard_map.131 = bf16[256,768]{1,0:T(8,128)(2,1)} custom-call(bf16[5,256,256]{2,1,0:T(8,128)(2,1)S(1)} %shard_map.128.adj.r_0_, bf16[256,768]{1,0:T(8,128)(2,1)S(1)} %shard_map.130.r_1_, bf16[256,768]{1,0:T(8,128)(2,1)} %collective-permute-done.4.r_2_, bf16[256,768]{1,0:T(8,128)(2,1)} %collective-permute-done.5.r_3_, ...), custom_call_target="tpu_custom_call" | custom-call | flops 805306368 | bytes 3825664 | tf_op jit(solution)/shard_map/pallas_call | solution.py:58
  81.5 2.8 %all-to-all-done.2 = f32[32,8,128]{2,1,0:T(8,128)S(1)} async-done(((f32[32,8,128]{2,1,0:T(8,128)}), f32[32,8,128]{2,1,0:T(8,128)S(1)}, u32[]{:S(2)}, u32[]{:S(2)}) %all-to-all-start.2) | async-done | bytes 131104 | tf_op jit(solution)/shard_map/all_to_all | solution.py:335
  84.3 0.7 shard_map.137
  (2 shorter events, 0.0 us)
Async XLA Ops:
  0.6 0.7 copy-start.6
  0.6 0.7 copy-start.5
  1.3 1.0 %copy-start.3 = (bf16[12,128,128]{2,1,0:T(8,128)(2,1)S(1)}, bf16[12,128,128]{2,1,0:T(8,128)(2,1)}, u32[]{:S(2)}) copy-start(bf16[12,128,128]{2,1,0:T(8,128)(2,1)} %tiles.1) | copy-start | bytes 1179652
  2.3 1.0 %copy-start.1 = (bf16[256,768]{1,0:T(8,128)(2,1)S(1)}, bf16[256,768]{1,0:T(8,128)(2,1)}, u32[]{:S(2)}) copy-start(bf16[256,768]{1,0:T(8,128)(2,1)} %r_0_.5) | copy-start | bytes 1179652
  3.3 7.1 %copy-start = (bf16[256,768]{1,0:T(8,128)(2,1)S(1)}, bf16[256,768]{1,0:T(8,128)(2,1)}, u32[]{:S(2)}) copy-start(bf16[256,768]{1,0:T(8,128)(2,1)} %r_0_.4) | copy-start | bytes 1179652
  3.3 7.1 %copy-start.2 = (bf16[3,64,64]{2,1,0:T(8,128)(2,1)S(1)}, bf16[3,64,64]{2,1,0:T(8,128)(2,1)}, u32[]{:S(2)}) copy-start(bf16[3,64,64]{2,1,0:T(8,128)(2,1)} %r_11_.1) | copy-start | bytes 73732
  3.3 7.1 %copy-start.4 = (bf16[2,64,128]{2,1,0:T(8,128)(2,1)S(1)}, bf16[2,64,128]{2,1,0:T(8,128)(2,1)}, u32[]{:S(2)}) copy-start(bf16[2,64,128]{2,1,0:T(8,128)(2,1)} %r_2_.1) | copy-start | bytes 98308
  4.1 8.3 %collective-permute-start.8 = (bf16[256,768]{1,0:T(8,128)(2,1)S(1)}, bf16[256,768]{1,0:T(8,128)(2,1)S(1)}, u32[]{:S(2)}, u32[]{:S(2)}) collective-permute-start(bf16[256,768]{1,0:T(8,128)(2,1)S(1)} %get-tuple-element.30), channel_id=1, source_target_pairs={{0,1},{1,0},{2,3},{3,2},{4,5},{5,4},{6,7},{7,6},{8,9},{9,8},{10,11... | collective-permute-start | bytes 1179656 | tf_op jit(solution)/shard_map/ppermute | solution.py:38
  7.4 11.5 %collective-permute-start.9 = (bf16[256,768]{1,0:T(8,128)(2,1)S(1)}, bf16[256,768]{1,0:T(8,128)(2,1)S(1)}, u32[]{:S(2)}, u32[]{:S(2)}) collective-permute-start(bf16[256,768]{1,0:T(8,128)(2,1)S(1)} %get-tuple-element.31), channel_id=1, source_target_pairs={{0,63},{1,2},{2,1},{3,4},{4,3},{5,6},{6,5},{7,8},{8,7},{9,10},{10,... | collective-permute-start | bytes 1179656 | tf_op jit(solution)/shard_map/ppermute | solution.py:38
  7.4 12.3 %collective-permute-start.10 = (bf16[256,768]{1,0:T(8,128)(2,1)S(1)}, bf16[256,768]{1,0:T(8,128)(2,1)S(1)}, u32[]{:S(2)}, u32[]{:S(2)}) collective-permute-start(bf16[256,768]{1,0:T(8,128)(2,1)S(1)} %get-tuple-element.32), channel_id=1, source_target_pairs={{0,64},{64,0},{128,192},{192,128},{1,65},{65,1},{129,193},{193,129... | collective-permute-start | bytes 1179656 | tf_op jit(solution)/shard_map/ppermute | solution.py:38
  8.6 1.9 %copy-start.7 = (f32[128]{0:T(128)S(1)}, f32[128]{0:T(128)}, u32[]{:S(2)}) copy-start(f32[128]{0:T(128)} %param.12) | copy-start | bytes 1540
  8.6 11.1 %collective-permute-start.11 = (bf16[256,768]{1,0:T(8,128)(2,1)S(1)}, bf16[256,768]{1,0:T(8,128)(2,1)S(1)}, u32[]{:S(2)}, u32[]{:S(2)}) collective-permute-start(bf16[256,768]{1,0:T(8,128)(2,1)S(1)} %get-tuple-element.33), channel_id=1, source_target_pairs={{0,192},{64,128},{128,64},{192,0},{1,193},{65,129},{129,65},{193,1... | collective-permute-start | bytes 1179656 | tf_op jit(solution)/shard_map/ppermute | solution.py:38
  11.6 10.5 %collective-permute-start.3 = (bf16[256,768]{1,0:T(8,128)(2,1)S(1)}, bf16[256,768]{1,0:T(8,128)(2,1)S(1)}, u32[]{:S(2)}, u32[]{:S(2)}) collective-permute-start(bf16[256,768]{1,0:T(8,128)(2,1)S(1)} %get-tuple-element.26.own.r_7_.r_1_), channel_id=1, source_target_pairs={{0,63},{1,2},{2,1},{3,4},{4,3},{5,6},{6,5},{7,8},{8,7},{9,10},{10,... | collective-permute-start | bytes 1179656 | tf_op jit(solution)/shard_map/ppermute | solution.py:38
  12.4 11.7 %collective-permute-start.2 = (bf16[256,768]{1,0:T(8,128)(2,1)S(1)}, bf16[256,768]{1,0:T(8,128)(2,1)S(1)}, u32[]{:S(2)}, u32[]{:S(2)}) collective-permute-start(bf16[256,768]{1,0:T(8,128)(2,1)S(1)} %get-tuple-element.26.own.r_7_.r_1_), channel_id=1, source_target_pairs={{0,1},{1,0},{2,3},{3,2},{4,5},{5,4},{6,7},{7,6},{8,9},{9,8},{10,11... | collective-permute-start | bytes 1179656 | tf_op jit(solution)/shard_map/ppermute | solution.py:38
  18.9 12.4 %collective-permute-start.1 = (bf16[256,768]{1,0:T(8,128)(2,1)S(1)}, bf16[256,768]{1,0:T(8,128)(2,1)S(1)}, u32[]{:S(2)}, u32[]{:S(2)}) collective-permute-start(bf16[256,768]{1,0:T(8,128)(2,1)S(1)} %get-tuple-element.26.own.r_7_.r_1_), channel_id=1, source_target_pairs={{0,192},{64,128},{128,64},{192,0},{1,193},{65,129},{129,65},{193,1... | collective-permute-start | bytes 1179656 | tf_op jit(solution)/shard_map/ppermute | solution.py:38
  19.7 11.6 %collective-permute-start = (bf16[256,768]{1,0:T(8,128)(2,1)S(1)}, bf16[256,768]{1,0:T(8,128)(2,1)S(1)}, u32[]{:S(2)}, u32[]{:S(2)}) collective-permute-start(bf16[256,768]{1,0:T(8,128)(2,1)S(1)} %get-tuple-element.26.own.r_7_.r_1_), channel_id=1, source_target_pairs={{0,64},{64,0},{128,192},{192,128},{1,65},{65,1},{129,193},{193,129... | collective-permute-start | bytes 1179656 | tf_op jit(solution)/shard_map/ppermute | solution.py:38
  20.6 15.6 %collective-permute-start.12 = (bf16[256,768]{1,0:T(8,128)(2,1)S(1)}, bf16[256,768]{1,0:T(8,128)(2,1)S(1)}, u32[]{:S(2)}, u32[]{:S(2)}) collective-permute-start(bf16[256,768]{1,0:T(8,128)(2,1)S(1)} %get-tuple-element.35), channel_id=1, source_target_pairs={{0,64},{64,0},{128,192},{192,128},{1,65},{65,1},{129,193},{193,129... | collective-permute-start | bytes 1179656 | tf_op jit(solution)/shard_map/ppermute | solution.py:38
  22.1 17.6 %collective-permute-start.13 = (bf16[256,768]{1,0:T(8,128)(2,1)S(1)}, bf16[256,768]{1,0:T(8,128)(2,1)S(1)}, u32[]{:S(2)}, u32[]{:S(2)}) collective-permute-start(bf16[256,768]{1,0:T(8,128)(2,1)S(1)} %get-tuple-element.36), channel_id=1, source_target_pairs={{0,192},{64,128},{128,64},{192,0},{1,193},{65,129},{129,65},{193,1... | collective-permute-start | bytes 1179656 | tf_op jit(solution)/shard_map/ppermute | solution.py:38
  24.0 18.7 %collective-permute-start.14 = (bf16[256,768]{1,0:T(8,128)(2,1)S(1)}, bf16[256,768]{1,0:T(8,128)(2,1)S(1)}, u32[]{:S(2)}, u32[]{:S(2)}) collective-permute-start(bf16[256,768]{1,0:T(8,128)(2,1)S(1)} %get-tuple-element.37), channel_id=1, source_target_pairs={{0,1},{1,0},{2,3},{3,2},{4,5},{5,4},{6,7},{7,6},{8,9},{9,8},{10,11... | collective-permute-start | bytes 1179656 | tf_op jit(solution)/shard_map/ppermute | solution.py:38
  31.3 11.4 %collective-permute-start.15 = (bf16[256,768]{1,0:T(8,128)(2,1)S(1)}, bf16[256,768]{1,0:T(8,128)(2,1)S(1)}, u32[]{:S(2)}, u32[]{:S(2)}) collective-permute-start(bf16[256,768]{1,0:T(8,128)(2,1)S(1)} %get-tuple-element.38), channel_id=1, source_target_pairs={{0,63},{1,2},{2,1},{3,4},{4,3},{5,6},{6,5},{7,8},{8,7},{9,10},{10,... | collective-permute-start | bytes 1179656 | tf_op jit(solution)/shard_map/ppermute | solution.py:38
  32.0 46.1 %collective-permute-start.7 = (bf16[256,768]{1,0:T(8,128)(2,1)S(1)}, bf16[256,768]{1,0:T(8,128)(2,1)}, u32[]{:S(2)}, u32[]{:S(2)}) collective-permute-start(bf16[256,768]{1,0:T(8,128)(2,1)S(1)} %shard_map.130.r_1_), channel_id=1, source_target_pairs={{0,63},{1,2},{2,1},{3,4},{4,3},{5,6},{6,5},{7,8},{8,7},{9,10},{10,... | collective-permute-start | bytes 1179656 | tf_op jit(solution)/shard_map/ppermute | solution.py:38
  36.1 42.0 %collective-permute-start.6 = (bf16[256,768]{1,0:T(8,128)(2,1)S(1)}, bf16[256,768]{1,0:T(8,128)(2,1)}, u32[]{:S(2)}, u32[]{:S(2)}) collective-permute-start(bf16[256,768]{1,0:T(8,128)(2,1)S(1)} %shard_map.130.r_1_), channel_id=1, source_target_pairs={{0,1},{1,0},{2,3},{3,2},{4,5},{5,4},{6,7},{7,6},{8,9},{9,8},{10,11... | collective-permute-start | bytes 1179656 | tf_op jit(solution)/shard_map/ppermute | solution.py:38
  39.7 38.4 %collective-permute-start.5 = (bf16[256,768]{1,0:T(8,128)(2,1)S(1)}, bf16[256,768]{1,0:T(8,128)(2,1)}, u32[]{:S(2)}, u32[]{:S(2)}) collective-permute-start(bf16[256,768]{1,0:T(8,128)(2,1)S(1)} %shard_map.130.r_1_), channel_id=1, source_target_pairs={{0,192},{64,128},{128,64},{192,0},{1,193},{65,129},{129,65},{193,1... | collective-permute-start | bytes 1179656 | tf_op jit(solution)/shard_map/ppermute | solution.py:38
  42.8 35.4 %collective-permute-start.4 = (bf16[256,768]{1,0:T(8,128)(2,1)S(1)}, bf16[256,768]{1,0:T(8,128)(2,1)}, u32[]{:S(2)}, u32[]{:S(2)}) collective-permute-start(bf16[256,768]{1,0:T(8,128)(2,1)S(1)} %shard_map.130.r_1_), channel_id=1, source_target_pairs={{0,64},{64,0},{128,192},{192,128},{1,65},{65,1},{129,193},{193,129... | collective-permute-start | bytes 1179656 | tf_op jit(solution)/shard_map/ppermute | solution.py:38
  70.6 13.7 %all-to-all-start.2 = ((f32[32,8,128]{2,1,0:T(8,128)}), f32[32,8,128]{2,1,0:T(8,128)S(1)}, u32[]{:S(2)}, u32[]{:S(2)}) async-start(f32[32,8,128]{2,1,0:T(8,128)} %shard_map.136), calls=%async_computation.2 | async-start | bytes 262144 | tf_op jit(solution)/shard_map/all_to_all | solution.py:335
